TPU v7x, 512 devices: a whole 4x8x8 slice. The times are simulated.
512 devices in a mesh: rep: 16 (over z_hi, y), dp: 32 (over x, z_lo, core).
Axes of the slice: x: 4, y: 8, z: 8 (z_hi: 2, z_lo: 4; z = z_hi * 4 + z_lo), core: 2. Of those that a mesh axis runs over, the one named last changes fastest.
Arguments:
- old_master: float32 [16, 512, 128], P('rep'), may hold values from -0.6 to 0.6
- old_first: float32 [16, 512, 128], P('rep'), may hold values from -6 to 6
- old_second: float32 [16, 512, 128], P('rep'), may hold values from 0.1 to 4
- grad_parts: bfloat16 [16, 32, 4096, 128], P('rep', 'dp'), may hold values from -0.3984375 to 0.3984375
- section_rows: int32 [16], replicated, may hold values from 1 to 512, 4096 in all
- adam_step: int32 [1], replicated, may hold values from 1 to 63
Outputs:
- new_master: float32 [4096, 128], P('dp')
- new_first: float32 [4096, 128], P('dp')
- new_second: float32 [4096, 128], P('dp')
- direction: float32 [4096, 128], P('dp')
Inputs may be any that keep to these rules, and one draw needn't show every extreme that they name: `section_rows`: lengths of the sections, summing to 4096; some section has exactly 512 rows.
All inputs are finite; a program needn't handle non-finite values.
Results may differ from a plain program's by a relative error of at most 0.0003.
Values sent between devices are 32-bit elements; how exact they have to be, the bound alone decides.
No kernel may reach another device: no remote copies, remote signals or barrier semaphores. Data moves between devices by JAX's collectives and lax.ppermute only.
A program may use at most 64 MiB of HBM per device.

v0:
```python
import jax
import jax.numpy as jnp
from jax import lax
from jax.sharding import PartitionSpec as P

BETA_ONE = 0.9
BETA_TWO = 0.999
EPSILON = 1e-08
RATE = 0.01
DECAY = 0.1


def take_rows(old_block, section_rows, shard_rows):
    rank_rep = lax.axis_index("rep")
    rank_dp = lax.axis_index("dp")
    section_ends = jnp.cumsum(section_rows)
    section_begins = section_ends - section_rows
    first_row = rank_dp * shard_rows - section_begins[rank_rep]
    section_len = section_rows[rank_rep]
    capacity = old_block.shape[1]
    padded = jnp.pad(old_block[0], ((shard_rows, shard_rows), (0, 0)))
    begin_row = jnp.clip(first_row + shard_rows, 0, capacity + shard_rows)
    window = lax.dynamic_slice_in_dim(padded, begin_row, shard_rows, 0)
    positions = first_row + jnp.arange(shard_rows, dtype=jnp.int32)
    usable = (positions >= 0) & (positions < section_len)
    return jnp.where(usable[:, None], window, 0.0)


def adam_update(master, first, second, gradient, adam_step):
    counted = adam_step[0].astype(jnp.float32)
    new_first = BETA_ONE * first + (1.0 - BETA_ONE) * gradient
    new_second = BETA_TWO * second + (1.0 - BETA_TWO) * gradient * gradient
    first_fix = 1.0 - jnp.power(jnp.float32(BETA_ONE), counted)
    second_fix = 1.0 - jnp.power(jnp.float32(BETA_TWO), counted)
    direction = new_first / first_fix / (jnp.sqrt(new_second / second_fix) + EPSILON)
    new_master = master - RATE * (direction + DECAY * master)
    return (new_master, new_first, new_second, direction)


def local(old_master, old_first, old_second, grad_parts, section_rows, adam_step):
    total_rows = grad_parts.shape[2]
    shard_rows = total_rows // lax.axis_size("dp")
    master = take_rows(old_master, section_rows, shard_rows)
    first = take_rows(old_first, section_rows, shard_rows)
    second = take_rows(old_second, section_rows, shard_rows)
    partial_grad = grad_parts[0, 0].astype(jnp.float32)
    grad_shard = lax.psum_scatter(partial_grad, "dp", scatter_dimension=0, tiled=True)
    master, first, second, gradient = lax.psum((master, first, second, grad_shard), "rep")
    return adam_update(master, first, second, gradient, adam_step)


def solution(mesh):
    in_specs = (
        P("rep", None, None),
        P("rep", None, None),
        P("rep", None, None),
        P("rep", "dp", None, None),
        P(),
        P(),
    )
    out_specs = (P("dp", None), P("dp", None), P("dp", None), P("dp", None))
    return jax.shard_map(local, mesh=mesh, in_specs=in_specs, out_specs=out_specs, check_vma=False)
```

profile of v0, /device:TPU:2, one launch (start us, length us, event | category | flops | bytes accessed | tf_op | source)
XLA Modules:
  0.0 369.3 jit_solution(15773558876252484877)
XLA Ops:
  7.2 0.0 copy-start.3
  7.2 0.0 copy-start.2
  7.2 0.0 copy-start.1
  7.2 0.0 copy-start
  7.2 0.0 reduce-scatter.2.cloned.1.call-start
  7.3 2.8 bitcast_convert_fusion
  10.0 0.0 reduce-scatter.2.cloned.1.call-update
  10.0 0.0 all-reduce.6.cloned.1.call-start
  10.1 0.0 copy-done.3
  10.1 0.1 copy.11
  10.2 0.1 reduce
  10.3 0.6 dynamic_slice.20
  10.9 0.6 dynamic_slice.19
  12.2 0.7 compare_and_fusion
  12.8 0.0 copy-done.2
  12.8 0.0 copy-done.1
  12.9 0.0 copy-done
  12.9 0.8 fusion.3
  13.6 131.9 %reduce-scatter.2.cloned.1.call-done = f32[128,128]{1,0:T(8,128)} async-done(((f32[4096,128]{1,0:T(8,128)}), f32[128,128]{1,0:T(8,128)}) %reduce-scatter.2.cloned.1.call-update) | async-done | bytes 65552 | tf_op jit(solution)/shard_map/reduce_scatter | solution.py:47
  145.5 0.0 all-reduce.6.cloned.1.call-update
  146.2 214.6 %all-reduce.6.cloned.1.call-done = (f32[128,128]{1,0:T(8,128)}, f32[128,128]{1,0:T(8,128)}, f32[128,128]{1,0:T(8,128)}, f32[128,128]{1,0:T(8,128)}) async-done(((f32[128,128]{1,0:T(8,128)}, f32[128,128]{1,0:T(8,128)}, f32[128,128]{1,0:T(8,128)}, f32[128,128]{1,0:T(8,128)}), (f32[128,128]{1,0:T(8,128)}, f32[128,128]{1,0:T(8,128)}, f32[128,128]{1,0:T(8,128)}, ...) | async-done | bytes 262160 | tf_op jit(solution)/shard_map/psum | solution.py:48
  360.9 1.6 multiply_subtract_fusion
  (2 shorter events, 0.0 us)
Async XLA Ops:
  7.2 2.9 copy-start.3
  7.2 5.7 %copy-start.2 = (f32[1,512,128]{2,1,0:T(8,128)S(1)}, f32[1,512,128]{2,1,0:T(8,128)}, u32[]{:S(2)}) copy-start(f32[1,512,128]{2,1,0:T(8,128)} %param.6) | copy-start | bytes 786436
  7.2 5.7 %copy-start.1 = (f32[1,512,128]{2,1,0:T(8,128)S(1)}, f32[1,512,128]{2,1,0:T(8,128)}, u32[]{:S(2)}) copy-start(f32[1,512,128]{2,1,0:T(8,128)} %param.7) | copy-start | bytes 786436
  7.2 5.7 %copy-start = (f32[1,512,128]{2,1,0:T(8,128)S(1)}, f32[1,512,128]{2,1,0:T(8,128)}, u32[]{:S(2)}) copy-start(f32[1,512,128]{2,1,0:T(8,128)} %param.8) | copy-start | bytes 786436
  7.2 138.3 %reduce-scatter.2.cloned.1.call-start = ((), (), s32[]{:S(2)}) async-start(), calls=%async_computation.1 | async-start | bytes 2162688 | tf_op jit(solution)/shard_map/reduce_scatter | solution.py:47
  10.0 350.8 %all-reduce.6.cloned.1.call-start = ((), (), s32[]{:S(2)}) async-start(), calls=%async_computation.2 | async-start | bytes 524288 | tf_op jit(solution)/shard_map/psum | solution.py:48
Sparse Core Ops, SparseCore 0:
  10.8 134.5 reduce-scatter.1
  149.5 211.3 all-reduce.5
where the time goes:
time: 370 us; the launch traced here: 369 us
  waiting for transfers between devices  347 us (94%)
  between operations  15.5 us (4%)
  other arithmetic  5.99 us (2%)
    psum x1, waiting for transfers between devices, local(): lax.psum((master, first, second, grad_shard), 'rep')  215 us
    reduce_scatter x1, waiting for transfers between devices, local(): lax.psum_scatter(partial_grad, 'dp', scatter_dimension=0, tiled=True)  132 us
  transfers between devices with their start and end apart: 2, of which 2 were waited for; matrix products, arithmetic and copies ran while one was open for 1% of the time, Pallas kernels for 0%

commit v1 on v0

v1 whole, which is shorter than its diff:
```python
import jax
import jax.numpy as jnp
from jax import lax
from jax.sharding import PartitionSpec as P

BETA_ONE = 0.9
BETA_TWO = 0.999
EPSILON = 1e-08
RATE = 0.01
DECAY = 0.1
LANES = 128
BITS = (0, 1)


def dp_index(x, z_two, z_one, core):
    return x * 8 + z_two * 4 + z_one * 2 + core


def rep_index(z_hi, y_high, y_one):
    return z_hi * 8 + y_high * 2 + y_one


def flat_index(x, z_two, z_one, core, z_hi, y_high, y_one):
    return rep_index(z_hi, y_high, y_one) * 32 + dp_index(x, z_two, z_one, core)


SPREAD_GROUPS = [
    [flat_index(x, z_two, z_one, core, z_hi, y_high, y_one) for x in range(4) for z_one in BITS for y_one in BITS]
    for z_hi in BITS for y_high in range(4) for z_two in BITS for core in BITS
]
FAR_GROUPS = [
    [flat_index(x, z_two, z_one, core, z_hi, y_high, y_one) for z_two in BITS for z_hi in BITS for y_high in range(4)]
    for y_one in BITS for x in range(4) for z_one in BITS for core in BITS
]
GATHER_GROUPS = [
    [rep_index(z_hi, y_high, y_one) for y_one in BITS for y_high in range(4)] for z_hi in BITS
]
CORE_PAIRS = [(d, d ^ 1) for d in range(32)]
Y_PAIRS = [(r, r ^ 1) for r in range(16)]


def adam_update(master, first, second, gradient, adam_step):
    counted = adam_step[0].astype(jnp.float32)
    new_first = BETA_ONE * first + (1.0 - BETA_ONE) * gradient
    new_second = BETA_TWO * second + (1.0 - BETA_TWO) * gradient * gradient
    first_fix = 1.0 - jnp.power(jnp.float32(BETA_ONE), counted)
    second_fix = 1.0 - jnp.power(jnp.float32(BETA_TWO), counted)
    direction = new_first / first_fix / (jnp.sqrt(new_second / second_fix) + EPSILON)
    new_master = master - RATE * (direction + DECAY * master)
    return (new_master, new_first, new_second, direction)


def state_rows(sections, section_rows, rank_rep, first_shard, z_two):
    owners = jnp.arange(section_rows.shape[0], dtype=jnp.int32)
    begin = jnp.sum(jnp.where(owners < rank_rep, section_rows, 0))
    length = jnp.sum(jnp.where(owners == rank_rep, section_rows, 0))
    capacity = sections[0].shape[1]
    padded = [jnp.pad(section[0], ((128, 128), (0, 0))) for section in sections]
    chosen = []
    for other in BITS:
        first_row = (first_shard + other * 4) * 128 - begin
        start = jnp.clip(first_row + 128, 0, capacity + 128)
        positions = first_row + jnp.arange(128, dtype=jnp.int32)
        usable = ((positions >= 0) & (positions < length))[:, None]
        for section in padded:
            window = lax.dynamic_slice_in_dim(section, start, 128, 0)
            window = jnp.where(usable, window, 0.0).reshape(2, 4, 2, 8, LANES)
            chosen.append(lax.dynamic_index_in_dim(window, z_two, 2, keepdims=False))
    return jnp.stack(chosen).reshape(2, 3, 2, 4, 8, LANES)


def local(old_master, old_first, old_second, grad_parts, section_rows, adam_step):
    rank_rep = lax.axis_index("rep")
    rank_dp = lax.axis_index("dp")
    core = rank_dp % 2
    z_two = (rank_dp // 4) % 2
    y_one = rank_rep % 2
    parts = grad_parts.reshape(4, 2, 2, 2, 2, 64, LANES)
    parts = jnp.transpose(parts, (3, 0, 2, 4, 1, 5, 6))
    given = lax.dynamic_index_in_dim(parts, 1 - core, 0, keepdims=False).astype(jnp.float32)
    kept = lax.dynamic_index_in_dim(parts, core, 0, keepdims=False).astype(jnp.float32)
    taken = lax.ppermute(given, "dp", CORE_PAIRS)
    rows = state_rows((old_master, old_first, old_second), section_rows, rank_rep, rank_dp - z_two * 4, z_two)
    other_rows = lax.dynamic_index_in_dim(rows, 1 - y_one, 2, keepdims=False)
    own_rows = lax.dynamic_index_in_dim(rows, y_one, 2, keepdims=False)
    pair_rows = own_rows + lax.ppermute(other_rows, "rep", Y_PAIRS)
    spread = (kept + taken).reshape(16, 128, LANES)
    spread = lax.all_to_all(spread, ("rep", "dp"), 0, 0, axis_index_groups=SPREAD_GROUPS)
    near_sum = jnp.sum(spread, axis=0).reshape(2, 1, 4, 16, LANES)
    near_sum = jnp.broadcast_to(near_sum, (2, 2, 4, 16, LANES))
    state = jnp.transpose(pair_rows, (0, 2, 1, 3, 4)).reshape(2, 1, 4, 24, LANES)
    state = jnp.broadcast_to(state, (2, 2, 4, 24, LANES))
    far = jnp.concatenate([near_sum, state], axis=3).reshape(16, 40, LANES)
    far = lax.all_to_all(far, ("rep", "dp"), 0, 0, axis_index_groups=FAR_GROUPS)
    gradient = jnp.sum(far[:, :16], axis=0)
    state = jnp.sum(far[:, 16:].reshape(2, 8, 3, 8, LANES), axis=1)
    state = jnp.transpose(state, (1, 0, 2, 3)).reshape(3, 16, LANES)
    new = jnp.stack(adam_update(state[0], state[1], state[2], gradient, adam_step))
    new = jnp.broadcast_to(new[None], (8, 4, 16, LANES))
    new = lax.all_to_all(new, "rep", 0, 0, axis_index_groups=GATHER_GROUPS)
    return tuple(new[:, i].reshape(128, LANES) for i in range(4))


def solution(mesh):
    in_specs = (
        P("rep", None, None),
        P("rep", None, None),
        P("rep", None, None),
        P("rep", "dp", None, None),
        P(),
        P(),
    )
    out_specs = (P("dp", None), P("dp", None), P("dp", None), P("dp", None))
    return jax.shard_map(local, mesh=mesh, in_specs=in_specs, out_specs=out_specs, check_vma=False)
```

time: 370 us -> 76.9 us (0.21)
  the two profiles are of different devices: /device:TPU:2 before, /device:TPU:12 now
where the time goes in v1:
time: 76.9 us; the launch traced here: 76.5 us
  starting transfers between devices  25.8 us (34%)
  waiting for transfers between devices  24.7 us (32%)
  blocking collectives  16.8 us (22%)
  other arithmetic  3.7 us (5%)
  between operations  2.94 us (4%)
  local copies, waits for them, and re-layouts  2.56 us (3%)
    all_to_all x1, blocking collectives, local(): new = lax.all_to_all(new, 'rep', 0, 0, axis_index_groups=GATHER_GROUPS)  16.8 us
    all_to_all x1, waiting for transfers between devices, local(): far = lax.all_to_all(far, ('rep', 'dp'), 0, 0, axis_index_groups=FAR_GROUPS)  13.3 us
    all_to_all x1, starting transfers between devices, local(): far = lax.all_to_all(far, ('rep', 'dp'), 0, 0, axis_index_groups=FAR_GROUPS)  12 us
    all_to_all x1, starting transfers between devices, local(): lax.all_to_all(spread, ('rep', 'dp'), 0, 0, axis_index_groups=SPREAD_GROUPS)  9.39 us
    ppermute x1, waiting for transfers between devices, local(): pair_rows = own_rows + lax.ppermute(other_rows, 'rep', Y_PAIRS)  8.76 us
    ppermute x1, waiting for transfers between devices, local(): taken = lax.ppermute(given, 'dp', CORE_PAIRS)  2.62 us
    ppermute x1, starting transfers between devices, local(): pair_rows = own_rows + lax.ppermute(other_rows, 'rep', Y_PAIRS)  2.46 us
    ppermute x1, starting transfers between devices, local(): taken = lax.ppermute(given, 'dp', CORE_PAIRS)  1.92 us
  transfers between devices with their start and end apart: 4, of which 3 were waited for; matrix products, arithmetic and copies ran while one was open for 2% of the time, Pallas kernels for 0%

profile of v1, /device:TPU:12, one launch (start us, length us, event | category | flops | bytes accessed | tf_op | source)
XLA Modules:
  0.0 76.5 jit_solution(6649028247488973282)
XLA Ops:
  0.6 0.0 copy-start
  0.7 1.2 %convert_bitcast_fusion = f32[4,2,2,2,64,128]{5,4,2,1,3,0:T(8,128)S(1)} fusion(bf16[4,2,2,2,2,64,128]{6,5,4,3,2,1,0:T(8,128)(2,1)} %bitcast.89, s32[]{:T(128)S(6)} %select_n.76), kind=kLoop, calls=%fused_computation.1 | loop fusion | flops 262144 | bytes 1572868 | tf_op jit(solution)/shard_map/convert_element_type | solution.py:80
  1.9 1.9 %collective-permute-start = (f32[4,2,2,2,64,128]{5,4,2,1,3,0:T(8,128)S(1)}, f32[4,2,2,2,64,128]{5,4,2,1,3,0:T(8,128)S(1)}, u32[]{:S(2)}, u32[]{:S(2)}) collective-permute-start(f32[4,2,2,2,64,128]{5,4,2,1,3,0:T(8,128)S(1)} %convert_bitcast_fusion), channel_id=1, source_target_pairs={{0,1},{1,0},{2,3},{3,2},{4,5},{5,4},{6,7},{7,6},{8,9},{9,8},{10,11... | collective-permute-start | bytes 3145736 | tf_op jit(solution)/shard_map/ppermute | solution.py:82
  3.8 2.6 %collective-permute-done = f32[4,2,2,2,64,128]{5,4,2,1,3,0:T(8,128)S(1)} collective-permute-done((f32[4,2,2,2,64,128]{5,4,2,1,3,0:T(8,128)S(1)}, f32[4,2,2,2,64,128]{5,4,2,1,3,0:T(8,128)S(1)}, u32[]{:S(2)}, u32[]{:S(2)}) %collective-permute-start) | collective-permute-done | bytes 1048608 | tf_op jit(solution)/shard_map/ppermute | solution.py:82
  6.5 0.0 copy-done
  6.5 0.2 bitcast_add_fusion
  6.6 1.1 %copy.38 = f32[4,2,2,2,64,128]{5,4,3,2,1,0:T(8,128)} copy(f32[4,2,2,2,64,128]{5,4,2,1,3,0:T(8,128)S(1)} %bitcast_add_fusion) | data formatting | bytes 2097152 | tf_op jit(solution)/shard_map/add | solution.py:87
  7.7 9.4 %all-to-all-start = ((f32[16,128,128]{2,1,0:T(8,128)}), f32[16,128,128]{2,1,0:T(8,128)S(1)}, u32[]{:S(2)}, u32[]{:S(2)}) async-start(f32[16,128,128]{2,1,0:T(8,128)} %bitcast.5), calls=%async_computation | async-start | bytes 2097152 | tf_op jit(solution)/shard_map/all_to_all | solution.py:88
  17.1 0.6 copy-done.4
  17.7 0.6 fusion.12
  19.7 0.7 compare_and_fusion
  20.4 0.0 copy-done.1
  20.4 0.0 copy-done.2
  20.4 0.0 copy-done.3
  20.4 0.1 fusion.2
  20.7 2.5 %collective-permute-start.1 = (f32[2,3,4,8,128]{4,3,2,1,0:T(8,128)S(1)}, f32[2,3,4,8,128]{4,3,2,1,0:T(8,128)S(1)}, u32[]{:S(2)}, u32[]{:S(2)}) collective-permute-start(f32[2,3,4,8,128]{4,3,2,1,0:T(8,128)S(1)} %dynamic-slice_bitcast_fusion), channel_id=1, source_target_pairs={{0,32},{32,0},{64,96},{96,64},{128,160},{160,128},{192,224},{224,1... | collective-permute-start | bytes 294920 | tf_op jit(solution)/shard_map/ppermute | solution.py:86
  23.1 8.8 %collective-permute-done.1 = f32[2,3,4,8,128]{4,3,2,1,0:T(8,128)S(1)} collective-permute-done((f32[2,3,4,8,128]{4,3,2,1,0:T(8,128)S(1)}, f32[2,3,4,8,128]{4,3,2,1,0:T(8,128)S(1)}, u32[]{:S(2)}, u32[]{:S(2)}) %collective-permute-start.1) | collective-permute-done | bytes 98336 | tf_op jit(solution)/shard_map/ppermute | solution.py:86
  31.9 0.0 all-to-all-done
  31.9 0.1 reduce_sum.47
  32.0 0.7 pad_maximum_fusion
  32.8 12.0 %all-to-all-start.1 = ((f32[16,40,128]{2,1,0:T(8,128)}), f32[16,40,128]{2,1,0:T(8,128)S(1)}, u32[]{:S(2)}, u32[]{:S(2)}) async-start(f32[16,40,128]{2,1,0:T(8,128)} %bitcast.27), calls=%async_computation.1 | async-start | bytes 655360 | tf_op jit(solution)/shard_map/all_to_all | solution.py:94
  45.5 13.3 %all-to-all-done.1 = f32[16,40,128]{2,1,0:T(8,128)S(1)} async-done(((f32[16,40,128]{2,1,0:T(8,128)}), f32[16,40,128]{2,1,0:T(8,128)S(1)}, u32[]{:S(2)}, u32[]{:S(2)}) %all-to-all-start.1) | async-done | bytes 327712 | tf_op jit(solution)/shard_map/all_to_all | solution.py:94
  59.0 16.8 %all_to_all.15 = f32[8,4,16,128]{3,2,1,0:T(8,128)S(1)} all-to-all(f32[8,4,16,128]{3,2,1,0:T(8,128)S(1)} %broadcast_in_dim.69), channel_id=1, replica_groups={{0,64,128,192,32,96,160,224},{256,320,384,448,288,352,416,480},{1,65,12..., dimensions={0} | all-to-all | bytes 524288 | tf_op jit(solution)/shard_map/all_to_all | solution.py:100
  75.8 0.7 fusion.15
  (20 shorter events, 0.2 us)
Async XLA Ops:
  0.6 5.8 %copy-start = (bf16[1,1,4096,128]{3,2,1,0:T(8,128)(2,1)S(1)}, bf16[1,1,4096,128]{3,2,1,0:T(8,128)(2,1)}, u32[]{:S(2)}) copy-start(bf16[1,1,4096,128]{3,2,1,0:T(8,128)(2,1)} %param.9) | copy-start | bytes 3145732
  1.9 4.6 %collective-permute-start = (f32[4,2,2,2,64,128]{5,4,2,1,3,0:T(8,128)S(1)}, f32[4,2,2,2,64,128]{5,4,2,1,3,0:T(8,128)S(1)}, u32[]{:S(2)}, u32[]{:S(2)}) collective-permute-start(f32[4,2,2,2,64,128]{5,4,2,1,3,0:T(8,128)S(1)} %convert_bitcast_fusion), channel_id=1, source_target_pairs={{0,1},{1,0},{2,3},{3,2},{4,5},{5,4},{6,7},{7,6},{8,9},{9,8},{10,11... | collective-permute-start | bytes 3145736 | tf_op jit(solution)/shard_map/ppermute | solution.py:82
  7.7 12.7 %copy-start.1 = (f32[1,512,128]{2,1,0:T(8,128)S(1)}, f32[1,512,128]{2,1,0:T(8,128)}, u32[]{:S(2)}) copy-start(f32[1,512,128]{2,1,0:T(8,128)} %param.6) | copy-start | bytes 786436
  7.7 12.7 %copy-start.2 = (f32[1,512,128]{2,1,0:T(8,128)S(1)}, f32[1,512,128]{2,1,0:T(8,128)}, u32[]{:S(2)}) copy-start(f32[1,512,128]{2,1,0:T(8,128)} %param.8) | copy-start | bytes 786436
  7.7 12.7 %copy-start.3 = (f32[1,512,128]{2,1,0:T(8,128)S(1)}, f32[1,512,128]{2,1,0:T(8,128)}, u32[]{:S(2)}) copy-start(f32[1,512,128]{2,1,0:T(8,128)} %param.7) | copy-start | bytes 786436
  7.7 24.2 %all-to-all-start = ((f32[16,128,128]{2,1,0:T(8,128)}), f32[16,128,128]{2,1,0:T(8,128)S(1)}, u32[]{:S(2)}, u32[]{:S(2)}) async-start(f32[16,128,128]{2,1,0:T(8,128)} %bitcast.5), calls=%async_computation | async-start | bytes 2097152 | tf_op jit(solution)/shard_map/all_to_all | solution.py:88
  17.1 0.7 copy-start.4
  20.7 11.2 %collective-permute-start.1 = (f32[2,3,4,8,128]{4,3,2,1,0:T(8,128)S(1)}, f32[2,3,4,8,128]{4,3,2,1,0:T(8,128)S(1)}, u32[]{:S(2)}, u32[]{:S(2)}) collective-permute-start(f32[2,3,4,8,128]{4,3,2,1,0:T(8,128)S(1)} %dynamic-slice_bitcast_fusion), channel_id=1, source_target_pairs={{0,32},{32,0},{64,96},{96,64},{128,160},{160,128},{192,224},{224,1... | collective-permute-start | bytes 294920 | tf_op jit(solution)/shard_map/ppermute | solution.py:86
  32.8 26.1 %all-to-all-start.1 = ((f32[16,40,128]{2,1,0:T(8,128)}), f32[16,40,128]{2,1,0:T(8,128)S(1)}, u32[]{:S(2)}, u32[]{:S(2)}) async-start(f32[16,40,128]{2,1,0:T(8,128)} %bitcast.27), calls=%async_computation.1 | async-start | bytes 655360 | tf_op jit(solution)/shard_map/all_to_all | solution.py:94

commit v2 on v1

v2 whole, which is shorter than its diff:
```python
import jax
import jax.numpy as jnp
from jax import lax
from jax.experimental import pallas as pl
from jax.experimental.pallas import tpu as pltpu
from jax.sharding import PartitionSpec as P

BETA_ONE = 0.9
BETA_TWO = 0.999
EPSILON = 1e-08
RATE = 0.01
DECAY = 0.1
LANES = 128
CAP = 512
SHARD = 128
PIECE = 16
EIGHT = 8
BITS = (0, 1)
VMEM = pl.BlockSpec(memory_space=pltpu.VMEM)


def dp_index(x, z_two, z_one, core):
    return x * 8 + z_two * 4 + z_one * 2 + core


def rep_index(z_hi, y_high, y_one):
    return z_hi * 8 + y_high * 2 + y_one


def flat_index(x, z_two, z_one, core, z_hi, y_high, y_one):
    return rep_index(z_hi, y_high, y_one) * 32 + dp_index(x, z_two, z_one, core)


SPREAD_GROUPS = [
    [flat_index(x, z_two, z_one, core, z_hi, y_high, y_one) for x in range(4) for z_one in BITS for y_one in BITS]
    for z_hi in BITS for y_high in range(4) for z_two in BITS for core in BITS
]
FAR_GROUPS = [
    [flat_index(x, z_two, z_one, core, z_hi, y_high, y_one) for z_two in BITS for z_hi in BITS for y_high in range(4)]
    for y_one in BITS for x in range(4) for z_one in BITS for core in BITS
]
GATHER_GROUPS = [
    [rep_index(z_hi, y_high, y_one) for y_one in BITS for y_high in range(4)] for z_hi in BITS
]
CORE_PAIRS = [(d, d ^ 1) for d in range(32)]


def adam_update(master, first, second, gradient, adam_step):
    counted = adam_step[0].astype(jnp.float32)
    new_first = BETA_ONE * first + (1.0 - BETA_ONE) * gradient
    new_second = BETA_TWO * second + (1.0 - BETA_TWO) * gradient * gradient
    first_fix = 1.0 - jnp.power(jnp.float32(BETA_ONE), counted)
    second_fix = 1.0 - jnp.power(jnp.float32(BETA_TWO), counted)
    direction = new_first / first_fix / (jnp.sqrt(new_second / second_fix) + EPSILON)
    new_master = master - RATE * (direction + DECAY * master)
    return (new_master, new_first, new_second, direction)


def state_kernel(rows_ref, master_ref, first_ref, second_ref, out_ref, held, sems):
    copies = [
        pltpu.make_async_copy(source.at[0], held.at[i, pl.ds(EIGHT, CAP)], sems.at[i])
        for i, source in enumerate((master_ref, first_ref, second_ref))
    ]
    for copy in copies:
        copy.start()
    rank_rep = lax.axis_index("rep")
    rank_dp = lax.axis_index("dp")
    core = rank_dp % 2
    z_one = (rank_dp // 2) % 2
    z_two = (rank_dp // 4) % 2
    turn = (rank_dp // 8) * 2 + z_one
    begin = jnp.int32(0)
    length = jnp.int32(0)
    for owner in range(16):
        held_rows = rows_ref[owner]
        begin += jnp.where(owner < rank_rep, held_rows, 0)
        length += jnp.where(owner == rank_rep, held_rows, 0)
    base = (turn // 4) * (4 * SHARD) + core * SHARD + (turn % 4) * PIECE + z_two * EIGHT - begin
    place = lax.broadcasted_iota(jnp.int32, (EIGHT, LANES), 0)
    for copy in copies:
        copy.wait()
    for peer in range(16):
        x, other_z, other_y = peer // 4, (peer // 2) % 2, peer % 2
        start = base + x * (8 * SHARD) + other_z * (2 * SHARD) + other_y * (SHARD // 2)
        usable = (place >= -start) & (place < length - start)
        at = jnp.clip(start, -EIGHT, CAP) + EIGHT
        for i in range(3):
            rows = held[i, pl.ds(at, EIGHT), :]
            out_ref[peer, i * EIGHT : (i + 1) * EIGHT, :] = jnp.where(usable, rows, 0.0)


def add_kernel(taken_ref, grad_ref, state_ref, out_ref):
    core = lax.axis_index("dp") % 2
    half = SHARD // 2
    for x in range(4):
        for z_two in BITS:
            for z_one in BITS:
                block = x * 4 + z_two * 2 + z_one
                own = pl.multiple_of((block * 2 + core) * SHARD, SHARD)
                total = taken_ref[pl.ds(block * SHARD, SHARD), :] + grad_ref[pl.ds(own, SHARD), :].astype(jnp.float32)
                for y_one in BITS:
                    peer = x * 4 + z_one * 2 + y_one
                    out_ref[peer, z_two * half : (z_two + 1) * half, :] = total[y_one * half : (y_one + 1) * half]
    out_ref[:, SHARD:, :] = state_ref[...]


def near_kernel(in_ref, out_ref):
    for z_two in BITS:
        for y_high in range(4):
            turn = z_two * 4 + y_high
            rows = pl.ds(turn * PIECE, PIECE)
            total = in_ref[0, rows, :]
            for peer in range(1, 16):
                total += in_ref[peer, rows, :]
            state = in_ref[2 * turn, SHARD:, :] + in_ref[2 * turn + 1, SHARD:, :]
            for z_hi in BITS:
                slot = z_two * 8 + z_hi * 4 + y_high
                out_ref[slot, :PIECE, :] = total
                out_ref[slot, PIECE:, :] = state


def local(old_master, old_first, old_second, grad_parts, section_rows, adam_step):
    core = lax.axis_index("dp") % 2
    grads = grad_parts.reshape(32 * SHARD, LANES)
    given = lax.dynamic_index_in_dim(grad_parts.reshape(16, 2, SHARD, LANES), 1 - core, 1, keepdims=False)
    taken = lax.ppermute(given.astype(jnp.float32).reshape(16 * SHARD, LANES), "dp", CORE_PAIRS)
    any_space = pl.BlockSpec(memory_space=pl.ANY)
    state = pl.pallas_call(
        state_kernel,
        out_shape=jax.ShapeDtypeStruct((16, 24, LANES), jnp.float32),
        in_specs=[pl.BlockSpec(memory_space=pltpu.SMEM), any_space, any_space, any_space],
        out_specs=VMEM,
        scratch_shapes=[pltpu.VMEM((3, CAP + 2 * EIGHT, LANES), jnp.float32), pltpu.SemaphoreType.DMA((3,))],
        cost_estimate=pl.CostEstimate(flops=100_000, bytes_accessed=1_000_000, transcendentals=0),
    )(section_rows, old_master, old_first, old_second)
    spread = pl.pallas_call(
        add_kernel,
        out_shape=jax.ShapeDtypeStruct((16, 152, LANES), jnp.float32),
        in_specs=[VMEM, VMEM, VMEM],
        out_specs=VMEM,
        compiler_params=pltpu.CompilerParams(vmem_limit_bytes=32 * 1024 * 1024),
    )(taken, grads, state)
    spread = lax.all_to_all(spread, ("rep", "dp"), 0, 0, axis_index_groups=SPREAD_GROUPS)
    far = pl.pallas_call(
        near_kernel,
        out_shape=jax.ShapeDtypeStruct((16, 40, LANES), jnp.float32),
        in_specs=[VMEM],
        out_specs=VMEM,
    )(spread)
    far = lax.all_to_all(far, ("rep", "dp"), 0, 0, axis_index_groups=FAR_GROUPS)
    gradient = jnp.sum(far[:, :PIECE], axis=0)
    state = jnp.sum(far[:, PIECE:].reshape(2, 8, 3, EIGHT, LANES), axis=1)
    state = jnp.transpose(state, (1, 0, 2, 3)).reshape(3, PIECE, LANES)
    new = jnp.stack(adam_update(state[0], state[1], state[2], gradient, adam_step))
    new = jnp.broadcast_to(new[None], (8, 4, PIECE, LANES))
    new = lax.all_to_all(new, "rep", 0, 0, axis_index_groups=GATHER_GROUPS)
    return tuple(new[:, i].reshape(SHARD, LANES) for i in range(4))


def solution(mesh):
    in_specs = (
        P("rep", None, None),
        P("rep", None, None),
        P("rep", None, None),
        P("rep", "dp", None, None),
        P(),
        P(),
    )
    out_specs = (P("dp", None), P("dp", None), P("dp", None), P("dp", None))
    return jax.shard_map(local, mesh=mesh, in_specs=in_specs, out_specs=out_specs, check_vma=False)
```

time: 76.9 us -> 78.9 us (1.026)
  the two profiles are of different devices: /device:TPU:12 before, /device:TPU:8 now
where the time goes in v2:
time: 78.9 us; the launch traced here: 78.4 us
  blocking collectives  40.9 us (52%)
  waiting for transfers between devices  14.2 us (18%)
  starting transfers between devices  14.1 us (18%)
  Pallas kernels  4.7 us (6%)
  local copies, waits for them, and re-layouts  2.75 us (3%)
  between operations  1.46 us (2%)
    all_to_all x1, blocking collectives, local(): lax.all_to_all(spread, ('rep', 'dp'), 0, 0, axis_index_groups=SPREAD_GROUPS)  27 us
    all_to_all x1, waiting for transfers between devices, local(): far = lax.all_to_all(far, ('rep', 'dp'), 0, 0, axis_index_groups=FAR_GROUPS)  14.1 us
    all_to_all x1, blocking collectives, local(): new = lax.all_to_all(new, 'rep', 0, 0, axis_index_groups=GATHER_GROUPS)  13.9 us
    all_to_all x1, starting transfers between devices, local(): far = lax.all_to_all(far, ('rep', 'dp'), 0, 0, axis_index_groups=FAR_GROUPS)  12.1 us
    pallas_call x1, Pallas kernels, local(): pl.pallas_call(state_kernel, out_shape=jax.ShapeDtypeStruct((16, 24, LANE...  2.5 us
    pallas_call x1, Pallas kernels, local(): pl.pallas_call(near_kernel, out_shape=jax.ShapeDtypeStruct((16, 40, LANES...  2.1 us
    ppermute x1, starting transfers between devices, local(): lax.ppermute(given.astype(jnp.float32).reshape(16 * SHARD, LANES), 'dp',...  2.05 us
  transfers between devices with their start and end apart: 2, of which 2 were waited for; matrix products, arithmetic and copies ran while one was open for 0% of the time, Pallas kernels for 3%

profile of v2, /device:TPU:8, one launch (start us, length us, event | category | flops | bytes accessed | tf_op | source)
XLA Modules:
  0.0 78.4 jit_solution(4344319656648046264)
XLA Ops:
  0.6 1.1 %constant_dynamic-slice_fusion = bf16[16,1,128,128]{3,2,1,0:T(8,128)(2,1)S(1)} fusion(bf16[16,2,128,128]{3,2,1,0:T(8,128)(2,1)} %bitcast.36, s32[]{:T(128)S(6)} %select_n.12), kind=kLoop, calls=%fused_computation.14 | loop fusion | bytes 1048580 | tf_op jit(solution)/shard_map/jit(dynamic_index_in_dim)/dynamic_slice | solution.py:125
  1.7 0.0 copy-start
  1.7 0.1 bitcast_convert_fusion
  1.9 2.1 %collective-permute-start = (f32[2048,128]{1,0:T(8,128)S(1)}, f32[2048,128]{1,0:T(8,128)S(1)}, u32[]{:S(2)}, u32[]{:S(2)}) collective-permute-start(f32[2048,128]{1,0:T(8,128)S(1)} %bitcast_convert_fusion), channel_id=1, source_target_pairs={{0,1},{1,0},{2,3},{3,2},{4,5},{5,4},{6,7},{7,6},{8,9},{9,8},{10,11... | collective-permute-start | bytes 3145736 | tf_op jit(solution)/shard_map/ppermute | solution.py:126
  3.9 2.5 %shard_map.93.state_ref = f32[16,24,128]{2,1,0:T(8,128)} custom-call(s32[16]{0:T(128)} %rows_ref.1, f32[1,512,128]{2,1,0:T(8,128)} %master_ref.1, f32[1,512,128]{2,1,0:T(8,128)} %first_ref.1, f32[1,512,128]{2,1,0:T(8,128)} %second_ref.1), custom_call_target="tpu_custom_call" | custom-call | flops 100000 | bytes 1000000 | tf_op jit(solution)/shard_map/pallas_call | solution.py:128
  6.4 0.1 collective-permute-done.taken_ref
  6.5 0.0 copy-done
  6.5 0.0 copy-start.1
  6.6 0.9 %copy-done.1 = f32[16,24,128]{2,1,0:T(8,128)S(1)} copy-done((f32[16,24,128]{2,1,0:T(8,128)S(1)}, f32[16,24,128]{2,1,0:T(8,128)}, u32[]{:S(2)}) %copy-start.1) | copy-done | bytes 196632
  7.5 0.1 shard_map.94
  7.6 27.0 %all_to_all.15.in_ref = f32[16,152,128]{2,1,0:T(8,128)} all-to-all(f32[16,152,128]{2,1,0:T(8,128)S(1)} %shard_map.94), channel_id=1, replica_groups={{0,32,2,34,8,40,10,42,16,48,18,50,24,56,26,58},{1,33,3,35,9,41,11,43,17..., dimensions={0} | all-to-all | bytes 2490368 | tf_op jit(solution)/shard_map/all_to_all | solution.py:143
  34.6 2.1 %shard_map.95 = f32[16,40,128]{2,1,0:T(8,128)} custom-call(f32[16,152,128]{2,1,0:T(8,128)} %all_to_all.15.in_ref), custom_call_target="tpu_custom_call" | custom-call | tf_op jit(solution)/shard_map/pallas_call | solution.py:144
  36.7 12.1 %all-to-all-start.1 = ((f32[16,40,128]{2,1,0:T(8,128)}), f32[16,40,128]{2,1,0:T(8,128)S(1)}, u32[]{:S(2)}, u32[]{:S(2)}) async-start(f32[16,40,128]{2,1,0:T(8,128)} %shard_map.95), calls=%async_computation.1 | async-start | bytes 655360 | tf_op jit(solution)/shard_map/all_to_all | solution.py:150
  49.5 14.1 %all-to-all-done.1 = f32[16,40,128]{2,1,0:T(8,128)S(1)} async-done(((f32[16,40,128]{2,1,0:T(8,128)}), f32[16,40,128]{2,1,0:T(8,128)S(1)}, u32[]{:S(2)}, u32[]{:S(2)}) %all-to-all-start.1) | async-done | bytes 327712 | tf_op jit(solution)/shard_map/all_to_all | solution.py:150
  63.8 13.9 %all_to_all.16 = f32[8,4,16,128]{3,2,1,0:T(8,128)S(1)} all-to-all(f32[8,4,16,128]{3,2,1,0:T(8,128)S(1)} %broadcast_in_dim.2), channel_id=1, replica_groups={{0,64,128,192,32,96,160,224},{256,320,384,448,288,352,416,480},{1,65,12..., dimensions={0} | all-to-all | bytes 524288 | tf_op jit(solution)/shard_map/all_to_all | solution.py:156
  77.7 0.7 fusion.6
  (6 shorter events, 0.1 us)
Async XLA Ops:
  1.7 4.8 %copy-start = (bf16[1,1,4096,128]{3,2,1,0:T(8,128)(2,1)S(1)}, bf16[1,1,4096,128]{3,2,1,0:T(8,128)(2,1)}, u32[]{:S(2)}) copy-start(bf16[1,1,4096,128]{3,2,1,0:T(8,128)(2,1)} %param.9) | copy-start | bytes 3145732
  1.9 4.7 %collective-permute-start = (f32[2048,128]{1,0:T(8,128)S(1)}, f32[2048,128]{1,0:T(8,128)S(1)}, u32[]{:S(2)}, u32[]{:S(2)}) collective-permute-start(f32[2048,128]{1,0:T(8,128)S(1)} %bitcast_convert_fusion), channel_id=1, source_target_pairs={{0,1},{1,0},{2,3},{3,2},{4,5},{5,4},{6,7},{7,6},{8,9},{9,8},{10,11... | collective-permute-start | bytes 3145736 | tf_op jit(solution)/shard_map/ppermute | solution.py:126
  6.5 0.9 %copy-start.1 = (f32[16,24,128]{2,1,0:T(8,128)S(1)}, f32[16,24,128]{2,1,0:T(8,128)}, u32[]{:S(2)}) copy-start(f32[16,24,128]{2,1,0:T(8,128)} %shard_map.93.state_ref) | copy-start | bytes 589828
  36.7 26.9 %all-to-all-start.1 = ((f32[16,40,128]{2,1,0:T(8,128)}), f32[16,40,128]{2,1,0:T(8,128)S(1)}, u32[]{:S(2)}, u32[]{:S(2)}) async-start(f32[16,40,128]{2,1,0:T(8,128)} %shard_map.95), calls=%async_computation.1 | async-start | bytes 655360 | tf_op jit(solution)/shard_map/all_to_all | solution.py:150

commit v3 on v2

--- a/solution.py
+++ b/solution.py
@@ -17,6 +17,7 @@
 EIGHT = 8
 BITS = (0, 1)
 VMEM = pl.BlockSpec(memory_space=pltpu.VMEM)
+SMALL = pltpu.CompilerParams(vmem_limit_bytes=8 * 1024 * 1024)
 
 
 def dp_index(x, z_two, z_one, core):
@@ -45,15 +46,15 @@
 CORE_PAIRS = [(d, d ^ 1) for d in range(32)]
 
 
-def adam_update(master, first, second, gradient, adam_step):
+def corrections(adam_step):
     counted = adam_step[0].astype(jnp.float32)
-    new_first = BETA_ONE * first + (1.0 - BETA_ONE) * gradient
-    new_second = BETA_TWO * second + (1.0 - BETA_TWO) * gradient * gradient
     first_fix = 1.0 - jnp.power(jnp.float32(BETA_ONE), counted)
     second_fix = 1.0 - jnp.power(jnp.float32(BETA_TWO), counted)
-    direction = new_first / first_fix / (jnp.sqrt(new_second / second_fix) + EPSILON)
-    new_master = master - RATE * (direction + DECAY * master)
-    return (new_master, new_first, new_second, direction)
+    return first_fix, second_fix
+
+
+def direction_of(new_first, new_second, first_fix, second_fix):
+    return new_first / first_fix / (jnp.sqrt(new_second / second_fix) + EPSILON)
 
 
 def state_kernel(rows_ref, master_ref, first_ref, second_ref, out_ref, held, sems):
@@ -131,14 +132,17 @@
         in_specs=[pl.BlockSpec(memory_space=pltpu.SMEM), any_space, any_space, any_space],
         out_specs=VMEM,
         scratch_shapes=[pltpu.VMEM((3, CAP + 2 * EIGHT, LANES), jnp.float32), pltpu.SemaphoreType.DMA((3,))],
+        compiler_params=SMALL,
         cost_estimate=pl.CostEstimate(flops=100_000, bytes_accessed=1_000_000, transcendentals=0),
     )(section_rows, old_master, old_first, old_second)
+    first_fix, second_fix = corrections(adam_step)
+    taken, first_fix, second_fix = lax.optimization_barrier((taken, first_fix, second_fix))
     spread = pl.pallas_call(
         add_kernel,
         out_shape=jax.ShapeDtypeStruct((16, 152, LANES), jnp.float32),
         in_specs=[VMEM, VMEM, VMEM],
         out_specs=VMEM,
-        compiler_params=pltpu.CompilerParams(vmem_limit_bytes=32 * 1024 * 1024),
+        compiler_params=SMALL,
     )(taken, grads, state)
     spread = lax.all_to_all(spread, ("rep", "dp"), 0, 0, axis_index_groups=SPREAD_GROUPS)
     far = pl.pallas_call(
@@ -146,15 +150,20 @@
         out_shape=jax.ShapeDtypeStruct((16, 40, LANES), jnp.float32),
         in_specs=[VMEM],
         out_specs=VMEM,
+        compiler_params=SMALL,
     )(spread)
     far = lax.all_to_all(far, ("rep", "dp"), 0, 0, axis_index_groups=FAR_GROUPS)
     gradient = jnp.sum(far[:, :PIECE], axis=0)
     state = jnp.sum(far[:, PIECE:].reshape(2, 8, 3, EIGHT, LANES), axis=1)
     state = jnp.transpose(state, (1, 0, 2, 3)).reshape(3, PIECE, LANES)
-    new = jnp.stack(adam_update(state[0], state[1], state[2], gradient, adam_step))
-    new = jnp.broadcast_to(new[None], (8, 4, PIECE, LANES))
-    new = lax.all_to_all(new, "rep", 0, 0, axis_index_groups=GATHER_GROUPS)
-    return tuple(new[:, i].reshape(SHARD, LANES) for i in range(4))
+    master, first, second = state
+    first = BETA_ONE * first + (1.0 - BETA_ONE) * gradient
+    second = BETA_TWO * second + (1.0 - BETA_TWO) * gradient * gradient
+    rows = jnp.broadcast_to(jnp.stack((master, first, second)), (8, 3, PIECE, LANES))
+    rows = lax.all_to_all(rows, "rep", 0, 0, axis_index_groups=GATHER_GROUPS)
+    master, first, second = (rows[:, i].reshape(SHARD, LANES) for i in range(3))
+    direction = direction_of(first, second, first_fix, second_fix)
+    return (master - RATE * (direction + DECAY * master), first, second, direction)
 
 
 def solution(mesh):

time: 78.9 us -> 73.6 us (0.933)
  blocking collectives: 40.9 us -> 65.6 us
  waiting for transfers between devices: 14.2 us -> 1.12 us
  starting transfers between devices: 14.1 us -> 2.05 us
  Pallas kernels: 4.7 us -> 0.9 us
  local copies, waits for them, and re-layouts: 2.75 us -> 1.23 us
    all_to_all x1 -> x2, blocking collectives: 13.9 us -> 39.6 us  [the longest x1 26.8 us: local(): far = lax.all_to_all(far, ('rep', 'dp'), 0, 0, axis_index_groups=FAR_GROUPS)]
    all_to_all x1 -> x0, waiting for transfers between devices: 14.1 us -> none  [local(): far = lax.all_to_all(far, ('rep', 'dp'), 0, 0, axis_index_groups=FAR_GROUPS)]
    all_to_all x1 -> x0, starting transfers between devices: 12.1 us -> none  [local(): far = lax.all_to_all(far, ('rep', 'dp'), 0, 0, axis_index_groups=FAR_GROUPS)]
    pallas_call x1, Pallas kernels: 2.1 us -> 0.07 us  [local(): pl.pallas_call(near_kernel, out_shape=jax.ShapeDtypeStruct((16, 40, LANES...]
    pallas_call x1, Pallas kernels: 2.5 us -> 0.73 us  [local(): pl.pallas_call(state_kernel, out_shape=jax.ShapeDtypeStruct((16, 24, LANE...]
    ppermute x1, waiting for transfers between devices: 0.12 us -> 1.12 us  [local(): lax.ppermute(given.astype(jnp.float32).reshape(16 * SHARD, LANES), 'dp',...]
    all_to_all x1, blocking collectives: 27 us -> 26 us  [local(): lax.all_to_all(spread, ('rep', 'dp'), 0, 0, axis_index_groups=SPREAD_GROUPS)]
    unnamed x4 -> x14, local copies, waits for them, and re-layouts: 0.93 us -> 0.04 us
  transfers between devices with their start and end apart: 2 -> 1, of which waited for: 2 -> 1; matrix products, arithmetic and copies ran while one was open for 0% -> 0% of each run, Pallas kernels for 3% -> 1%
where the time goes in v3:
time: 73.6 us; the launch traced here: 73.3 us
  blocking collectives  65.6 us (89%)
  starting transfers between devices  2.05 us (3%)
  between operations  1.55 us (2%)
  local copies, waits for them, and re-layouts  1.23 us (2%)
  waiting for transfers between devices  1.12 us (2%)
  Pallas kernels  0.9 us (1%)
  other arithmetic  0.87 us (1%)
    all_to_all x1, blocking collectives, local(): far = lax.all_to_all(far, ('rep', 'dp'), 0, 0, axis_index_groups=FAR_GROUPS)  26.8 us
    all_to_all x1, blocking collectives, local(): lax.all_to_all(spread, ('rep', 'dp'), 0, 0, axis_index_groups=SPREAD_GROUPS)  26 us
    all_to_all x1, blocking collectives, local(): rows = lax.all_to_all(rows, 'rep', 0, 0, axis_index_groups=GATHER_GROUPS)  12.8 us
    ppermute x1, starting transfers between devices, local(): lax.ppermute(given.astype(jnp.float32).reshape(16 * SHARD, LANES), 'dp',...  2.05 us
  transfers between devices with their start and end apart: 1, of which 1 were waited for; matrix products, arithmetic and copies ran while one was open for 0% of the time, Pallas kernels for 1%

profile of v3, /device:TPU:8, one launch (start us, length us, event | category | flops | bytes accessed | tf_op | source)
XLA Modules:
  0.0 73.3 jit_solution(1253899284047684440)
XLA Ops:
  0.6 0.0 copy-start.1
  0.7 0.0 copy-start.2
  0.7 0.0 copy-start.3
  0.7 0.0 copy-start.4
  0.7 1.2 %constant_dynamic-slice_fusion = bf16[16,1,128,128]{3,2,1,0:T(8,128)(2,1)S(1)} fusion(bf16[16,2,128,128]{3,2,1,0:T(8,128)(2,1)} %bitcast.39, s32[]{:T(128)S(6)} %select_n.12), kind=kLoop, calls=%fused_computation.17 | loop fusion | bytes 1048580 | tf_op jit(solution)/shard_map/jit(dynamic_index_in_dim)/dynamic_slice | solution.py:126
  1.8 0.0 copy-start
  1.9 0.1 bitcast_convert_fusion
  2.0 2.1 %collective-permute-start = (f32[2048,128]{1,0:T(8,128)S(1)}, f32[2048,128]{1,0:T(8,128)S(1)}, u32[]{:S(2)}, u32[]{:S(2)}) collective-permute-start(f32[2048,128]{1,0:T(8,128)S(1)} %bitcast_convert_fusion), channel_id=1, source_target_pairs={{0,1},{1,0},{2,3},{3,2},{4,5},{5,4},{6,7},{7,6},{8,9},{9,8},{10,11... | collective-permute-start | bytes 3145736 | tf_op jit(solution)/shard_map/ppermute | solution.py:127
  4.0 0.0 copy-done.1
  4.0 0.0 copy-done.2
  4.0 0.0 copy-done.3
  4.1 0.0 copy-done.4
  4.1 0.7 shard_map.93.state_ref
  5.5 1.1 %collective-permute-done.taken_ref = f32[2048,128]{1,0:T(8,128)S(1)} collective-permute-done((f32[2048,128]{1,0:T(8,128)S(1)}, f32[2048,128]{1,0:T(8,128)S(1)}, u32[]{:S(2)}, u32[]{:S(2)}) %collective-permute-start) | collective-permute-done | bytes 1048608 | tf_op jit(solution)/shard_map/ppermute | solution.py:127
  6.7 0.0 copy-done
  6.7 0.1 shard_map.94
  6.8 26.0 %all_to_all.15.in_ref = f32[16,152,128]{2,1,0:T(8,128)S(1)} all-to-all(f32[16,152,128]{2,1,0:T(8,128)S(1)} %shard_map.94), channel_id=1, replica_groups={{0,32,2,34,8,40,10,42,16,48,18,50,24,56,26,58},{1,33,3,35,9,41,11,43,17..., dimensions={0} | all-to-all | bytes 2490368 | tf_op jit(solution)/shard_map/all_to_all | solution.py:147
  32.8 0.1 shard_map.95
  32.9 26.8 %all_to_all.16 = f32[16,40,128]{2,1,0:T(8,128)S(1)} all-to-all(f32[16,40,128]{2,1,0:T(8,128)S(1)} %shard_map.95), channel_id=1, replica_groups={{0,64,128,192,256,320,384,448,4,68,132,196,260,324,388,452},{1,65,129,1..., dimensions={0} | all-to-all | bytes 655360 | tf_op jit(solution)/shard_map/all_to_all | solution.py:155
  59.8 12.8 %all_to_all.17 = f32[8,3,16,128]{3,2,1,0:T(8,128)S(1)} all-to-all(f32[8,3,16,128]{3,2,1,0:T(8,128)S(1)} %broadcast_in_dim.3), channel_id=1, replica_groups={{0,64,128,192,32,96,160,224},{256,320,384,448,288,352,416,480},{1,65,12..., dimensions={0} | all-to-all | bytes 393216 | tf_op jit(solution)/shard_map/all_to_all | solution.py:163
  72.6 0.0 copy-start.5
  72.6 0.0 copy-start.6
  72.6 0.7 bitcast_subtract_fusion
  73.3 0.0 copy-done.5
  (9 shorter events, 0.1 us)
Async XLA Ops:
  0.6 3.4 %copy-start.1 = (f32[1,512,128]{2,1,0:T(8,128)S(1)}, f32[1,512,128]{2,1,0:T(8,128)}, u32[]{:S(2)}) copy-start(f32[1,512,128]{2,1,0:T(8,128)} %master_ref.1) | copy-start | bytes 786436
  0.7 3.4 %copy-start.2 = (f32[1,512,128]{2,1,0:T(8,128)S(1)}, f32[1,512,128]{2,1,0:T(8,128)}, u32[]{:S(2)}) copy-start(f32[1,512,128]{2,1,0:T(8,128)} %first_ref.1) | copy-start | bytes 786436
  0.7 3.4 %copy-start.3 = (f32[1,512,128]{2,1,0:T(8,128)S(1)}, f32[1,512,128]{2,1,0:T(8,128)}, u32[]{:S(2)}) copy-start(f32[1,512,128]{2,1,0:T(8,128)} %second_ref.1) | copy-start | bytes 786436
  0.7 3.4 %copy-start.4 = (s32[16]{0:T(128)S(1)}, s32[16]{0:T(128)}, u32[]{:S(2)}) copy-start(s32[16]{0:T(128)} %rows_ref.1) | copy-start | bytes 196
  1.8 4.8 %copy-start = (bf16[1,1,4096,128]{3,2,1,0:T(8,128)(2,1)S(1)}, bf16[1,1,4096,128]{3,2,1,0:T(8,128)(2,1)}, u32[]{:S(2)}) copy-start(bf16[1,1,4096,128]{3,2,1,0:T(8,128)(2,1)} %param.9) | copy-start | bytes 3145732
  2.0 4.7 %collective-permute-start = (f32[2048,128]{1,0:T(8,128)S(1)}, f32[2048,128]{1,0:T(8,128)S(1)}, u32[]{:S(2)}, u32[]{:S(2)}) collective-permute-start(f32[2048,128]{1,0:T(8,128)S(1)} %bitcast_convert_fusion), channel_id=1, source_target_pairs={{0,1},{1,0},{2,3},{3,2},{4,5},{5,4},{6,7},{7,6},{8,9},{9,8},{10,11... | collective-permute-start | bytes 3145736 | tf_op jit(solution)/shard_map/ppermute | solution.py:127
  72.6 0.7 %copy-start.5 = (f32[8,1,16,128]{3,2,1,0:T(8,128)}, f32[8,1,16,128]{3,2,1,0:T(8,128)S(1)}, u32[]{:S(2)}) copy-start(f32[8,1,16,128]{3,2,1,0:T(8,128)S(1)} %get-tuple-element.12) | copy-start | bytes 196612
  72.6 0.7 %copy-start.6 = (f32[8,1,16,128]{3,2,1,0:T(8,128)}, f32[8,1,16,128]{3,2,1,0:T(8,128)S(1)}, u32[]{:S(2)}) copy-start(f32[8,1,16,128]{3,2,1,0:T(8,128)S(1)} %get-tuple-element.13) | copy-start | bytes 196612

commit v4 on v3

--- a/solution.py
+++ b/solution.py
@@ -1,3 +1,5 @@
+import itertools
+
 import jax
 import jax.numpy as jnp
 from jax import lax
@@ -32,16 +34,25 @@
     return rep_index(z_hi, y_high, y_one) * 32 + dp_index(x, z_two, z_one, core)
 
 
+SPREAD_X, SPREAD_Z, SPREAD_Y = (3, 2, 1, 0), (1, 0), (0, 1)
+FAR_TWO, FAR_Z, FAR_Y = (0, 1), (1, 0), (2, 3, 0, 1)
+GATHER_LOW, GATHER_HIGH = (0, 1), (2, 3, 0, 1)
+
+
+def spread_slot(x, z_one, y_one):
+    return SPREAD_X.index(x) * 4 + SPREAD_Z.index(z_one) * 2 + SPREAD_Y.index(y_one)
+
+
 SPREAD_GROUPS = [
-    [flat_index(x, z_two, z_one, core, z_hi, y_high, y_one) for x in range(4) for z_one in BITS for y_one in BITS]
+    [flat_index(x, z_two, z_one, core, z_hi, y_high, y_one) for x in SPREAD_X for z_one in SPREAD_Z for y_one in SPREAD_Y]
     for z_hi in BITS for y_high in range(4) for z_two in BITS for core in BITS
 ]
 FAR_GROUPS = [
-    [flat_index(x, z_two, z_one, core, z_hi, y_high, y_one) for z_two in BITS for z_hi in BITS for y_high in range(4)]
+    [flat_index(x, z_two, z_one, core, z_hi, y_high, y_one) for z_two in FAR_TWO for z_hi in FAR_Z for y_high in FAR_Y]
     for y_one in BITS for x in range(4) for z_one in BITS for core in BITS
 ]
 GATHER_GROUPS = [
-    [rep_index(z_hi, y_high, y_one) for y_one in BITS for y_high in range(4)] for z_hi in BITS
+    [rep_index(z_hi, y_high, y_one) for y_one in GATHER_LOW for y_high in GATHER_HIGH] for z_hi in BITS
 ]
 CORE_PAIRS = [(d, d ^ 1) for d in range(32)]
 
@@ -76,13 +87,14 @@
         held_rows = rows_ref[owner]
         begin += jnp.where(owner < rank_rep, held_rows, 0)
         length += jnp.where(owner == rank_rep, held_rows, 0)
-    base = (turn // 4) * (4 * SHARD) + core * SHARD + (turn % 4) * PIECE + z_two * EIGHT - begin
+    piece = sum(jnp.where(turn % 4 == y_high, GATHER_HIGH.index(y_high), 0) for y_high in range(4))
+    base = (turn // 4) * (4 * SHARD) + core * SHARD + piece * PIECE + z_two * EIGHT - begin
     place = lax.broadcasted_iota(jnp.int32, (EIGHT, LANES), 0)
     for copy in copies:
         copy.wait()
-    for peer in range(16):
-        x, other_z, other_y = peer // 4, (peer // 2) % 2, peer % 2
-        start = base + x * (8 * SHARD) + other_z * (2 * SHARD) + other_y * (SHARD // 2)
+    for x, other_z, other_y in itertools.product(range(4), BITS, BITS):
+        peer = spread_slot(x, other_z, other_y)
+        start = base + x * (8 * SHARD) + other_z * (2 * SHARD) + GATHER_LOW.index(other_y) * (SHARD // 2)
         usable = (place >= -start) & (place < length - start)
         at = jnp.clip(start, -EIGHT, CAP) + EIGHT
         for i in range(3):
@@ -100,8 +112,9 @@
                 own = pl.multiple_of((block * 2 + core) * SHARD, SHARD)
                 total = taken_ref[pl.ds(block * SHARD, SHARD), :] + grad_ref[pl.ds(own, SHARD), :].astype(jnp.float32)
                 for y_one in BITS:
-                    peer = x * 4 + z_one * 2 + y_one
-                    out_ref[peer, z_two * half : (z_two + 1) * half, :] = total[y_one * half : (y_one + 1) * half]
+                    peer = spread_slot(x, z_one, y_one)
+                    first = GATHER_LOW.index(y_one) * half
+                    out_ref[peer, z_two * half : (z_two + 1) * half, :] = total[first : first + half]
     out_ref[:, SHARD:, :] = state_ref[...]
 
 
@@ -109,13 +122,14 @@
     for z_two in BITS:
         for y_high in range(4):
             turn = z_two * 4 + y_high
-            rows = pl.ds(turn * PIECE, PIECE)
+            rows = pl.ds((z_two * 4 + GATHER_HIGH.index(y_high)) * PIECE, PIECE)
             total = in_ref[0, rows, :]
             for peer in range(1, 16):
                 total += in_ref[peer, rows, :]
-            state = in_ref[2 * turn, SHARD:, :] + in_ref[2 * turn + 1, SHARD:, :]
+            source = spread_slot(turn // 2, turn % 2, 0), spread_slot(turn // 2, turn % 2, 1)
+            state = in_ref[source[0], SHARD:, :] + in_ref[source[1], SHARD:, :]
             for z_hi in BITS:
-                slot = z_two * 8 + z_hi * 4 + y_high
+                slot = FAR_TWO.index(z_two) * 8 + z_hi * 4 + FAR_Y.index(y_high)
                 out_ref[slot, :PIECE, :] = total
                 out_ref[slot, PIECE:, :] = state
 
@@ -155,7 +169,7 @@
     far = lax.all_to_all(far, ("rep", "dp"), 0, 0, axis_index_groups=FAR_GROUPS)
     gradient = jnp.sum(far[:, :PIECE], axis=0)
     state = jnp.sum(far[:, PIECE:].reshape(2, 8, 3, EIGHT, LANES), axis=1)
-    state = jnp.transpose(state, (1, 0, 2, 3)).reshape(3, PIECE, LANES)
+    state = jnp.stack([state[FAR_TWO.index(z_two)] for z_two in BITS], axis=1).reshape(3, PIECE, LANES)
     master, first, second = state
     first = BETA_ONE * first + (1.0 - BETA_ONE) * gradient
     second = BETA_TWO * second + (1.0 - BETA_TWO) * gradient * gradient

time: 73.6 us -> 67.2 us (0.913)
  blocking collectives: 65.6 us -> 59.2 us
    all_to_all x1, blocking collectives: 26.8 us -> 21 us  [local(): far = lax.all_to_all(far, ('rep', 'dp'), 0, 0, axis_index_groups=FAR_GROUPS)]
where the time goes in v4:
time: 67.2 us; the launch traced here: 66.9 us
  blocking collectives  59.2 us (88%)
  starting transfers between devices  2.05 us (3%)
  between operations  1.56 us (2%)
  local copies, waits for them, and re-layouts  1.23 us (2%)
  waiting for transfers between devices  1.11 us (2%)
  Pallas kernels  0.9 us (1%)
  other arithmetic  0.88 us (1%)
    all_to_all x1, blocking collectives, local(): lax.all_to_all(spread, ('rep', 'dp'), 0, 0, axis_index_groups=SPREAD_GROUPS)  25.8 us
    all_to_all x1, blocking collectives, local(): far = lax.all_to_all(far, ('rep', 'dp'), 0, 0, axis_index_groups=FAR_GROUPS)  21 us
    all_to_all x1, blocking collectives, local(): rows = lax.all_to_all(rows, 'rep', 0, 0, axis_index_groups=GATHER_GROUPS)  12.4 us
    ppermute x1, starting transfers between devices, local(): lax.ppermute(given.astype(jnp.float32).reshape(16 * SHARD, LANES), 'dp',...  2.05 us
  transfers between devices with their start and end apart: 1, of which 1 were waited for; matrix products, arithmetic and copies ran while one was open for 0% of the time, Pallas kernels for 1%

profile of v4, /device:TPU:8, one launch (start us, length us, event | category | flops | bytes accessed | tf_op | source)
XLA Modules:
  0.0 66.9 jit_solution(6536358177482559259)
XLA Ops:
  0.6 0.0 copy-start.1
  0.7 0.0 copy-start.2
  0.7 0.0 copy-start.3
  0.7 0.0 copy-start.4
  0.7 1.2 %constant_dynamic-slice_fusion = bf16[16,1,128,128]{3,2,1,0:T(8,128)(2,1)S(1)} fusion(bf16[16,2,128,128]{3,2,1,0:T(8,128)(2,1)} %bitcast.44, s32[]{:T(128)S(6)} %select_n.12), kind=kLoop, calls=%fused_computation.26 | loop fusion | bytes 1048580 | tf_op jit(solution)/shard_map/jit(dynamic_index_in_dim)/dynamic_slice | solution.py:140
  1.8 0.0 copy-start
  1.9 0.1 bitcast_convert_fusion
  2.0 2.1 %collective-permute-start = (f32[2048,128]{1,0:T(8,128)S(1)}, f32[2048,128]{1,0:T(8,128)S(1)}, u32[]{:S(2)}, u32[]{:S(2)}) collective-permute-start(f32[2048,128]{1,0:T(8,128)S(1)} %bitcast_convert_fusion), channel_id=1, source_target_pairs={{0,1},{1,0},{2,3},{3,2},{4,5},{5,4},{6,7},{7,6},{8,9},{9,8},{10,11... | collective-permute-start | bytes 3145736 | tf_op jit(solution)/shard_map/ppermute | solution.py:141
  4.0 0.0 copy-done.1
  4.0 0.0 copy-done.2
  4.0 0.0 copy-done.3
  4.1 0.0 copy-done.4
  4.1 0.7 %shard_map.93.state_ref = f32[16,24,128]{2,1,0:T(8,128)S(1)} custom-call(s32[16]{0:T(128)S(1)} %copy-done.4, f32[1,512,128]{2,1,0:T(8,128)S(1)} %copy-done.1, f32[1,512,128]{2,1,0:T(8,128)S(1)} %copy-done.2, f32[1,512,128]{2,1,0:T(8,128)S(1)} %copy-done.3), custom_call_target="tpu_custom_call" | custom-call | flops 100000 | bytes 1000000 | tf_op jit(solution)/shard_map/pallas_call | solution.py:143
  5.5 1.1 %collective-permute-done.taken_ref = f32[2048,128]{1,0:T(8,128)S(1)} collective-permute-done((f32[2048,128]{1,0:T(8,128)S(1)}, f32[2048,128]{1,0:T(8,128)S(1)}, u32[]{:S(2)}, u32[]{:S(2)}) %collective-permute-start) | collective-permute-done | bytes 1048608 | tf_op jit(solution)/shard_map/ppermute | solution.py:141
  6.7 0.0 copy-done
  6.7 0.1 shard_map.94
  6.8 25.8 %all_to_all.15.in_ref = f32[16,152,128]{2,1,0:T(8,128)S(1)} all-to-all(f32[16,152,128]{2,1,0:T(8,128)S(1)} %shard_map.94), channel_id=1, replica_groups={{26,58,24,56,18,50,16,48,10,42,8,40,2,34,0,32},{27,59,25,57,19,51,17,49..., dimensions={0} | all-to-all | bytes 2490368 | tf_op jit(solution)/shard_map/all_to_all | solution.py:161
  32.5 0.1 shard_map.95
  32.6 21.0 %all_to_all.16 = f32[16,40,128]{2,1,0:T(8,128)S(1)} all-to-all(f32[16,40,128]{2,1,0:T(8,128)S(1)} %shard_map.95), channel_id=1, replica_groups={{384,448,256,320,128,192,0,64,388,452,260,324,132,196,4,68},{385,449,25..., dimensions={0} | all-to-all | bytes 655360 | tf_op jit(solution)/shard_map/all_to_all | solution.py:169
  53.7 12.4 %all_to_all.17 = f32[8,3,16,128]{3,2,1,0:T(8,128)S(1)} all-to-all(f32[8,3,16,128]{3,2,1,0:T(8,128)S(1)} %broadcast_in_dim.3), channel_id=1, replica_groups={{128,192,0,64,160,224,32,96},{384,448,256,320,416,480,288,352},{129,193..., dimensions={0} | all-to-all | bytes 393216 | tf_op jit(solution)/shard_map/all_to_all | solution.py:177
  66.2 0.0 copy-start.5
  66.2 0.0 copy-start.6
  66.2 0.7 %bitcast_subtract_fusion = (f32[128,128]{1,0:T(8,128)}, f32[128,128]{1,0:T(8,128)}) fusion(f32[8,1,16,128]{3,2,1,0:T(8,128)S(1)} %get-tuple-element.14, f32[]{:T(128)} %bitcast.3, f32[]{:T(128)} %bitcast.2, f32[8,1,16,128]{3,2,1,0:T(8,128)S(1)} %get-tuple-element.12, f32[8,1,16,128]{3,2,1,0:T(8,128)S(1)} %get-tuple-element.13), kind=kLoop, calls=%fused_computation.2 | loop fusion | flops 131072 | bytes 327688 | tf_op jit(solution)/shard_map/sub | solution.py:180
  66.9 0.0 copy-done.5
  (10 shorter events, 0.1 us)
Async XLA Ops:
  0.6 3.4 %copy-start.1 = (f32[1,512,128]{2,1,0:T(8,128)S(1)}, f32[1,512,128]{2,1,0:T(8,128)}, u32[]{:S(2)}) copy-start(f32[1,512,128]{2,1,0:T(8,128)} %master_ref.1) | copy-start | bytes 786436
  0.7 3.4 %copy-start.2 = (f32[1,512,128]{2,1,0:T(8,128)S(1)}, f32[1,512,128]{2,1,0:T(8,128)}, u32[]{:S(2)}) copy-start(f32[1,512,128]{2,1,0:T(8,128)} %first_ref.1) | copy-start | bytes 786436
  0.7 3.4 %copy-start.3 = (f32[1,512,128]{2,1,0:T(8,128)S(1)}, f32[1,512,128]{2,1,0:T(8,128)}, u32[]{:S(2)}) copy-start(f32[1,512,128]{2,1,0:T(8,128)} %second_ref.1) | copy-start | bytes 786436
  0.7 3.4 %copy-start.4 = (s32[16]{0:T(128)S(1)}, s32[16]{0:T(128)}, u32[]{:S(2)}) copy-start(s32[16]{0:T(128)} %rows_ref.1) | copy-start | bytes 196
  1.8 4.8 %copy-start = (bf16[1,1,4096,128]{3,2,1,0:T(8,128)(2,1)S(1)}, bf16[1,1,4096,128]{3,2,1,0:T(8,128)(2,1)}, u32[]{:S(2)}) copy-start(bf16[1,1,4096,128]{3,2,1,0:T(8,128)(2,1)} %param.9) | copy-start | bytes 3145732
  2.0 4.7 %collective-permute-start = (f32[2048,128]{1,0:T(8,128)S(1)}, f32[2048,128]{1,0:T(8,128)S(1)}, u32[]{:S(2)}, u32[]{:S(2)}) collective-permute-start(f32[2048,128]{1,0:T(8,128)S(1)} %bitcast_convert_fusion), channel_id=1, source_target_pairs={{0,1},{1,0},{2,3},{3,2},{4,5},{5,4},{6,7},{7,6},{8,9},{9,8},{10,11... | collective-permute-start | bytes 3145736 | tf_op jit(solution)/shard_map/ppermute | solution.py:141
  66.2 0.7 %copy-start.5 = (f32[8,1,16,128]{3,2,1,0:T(8,128)}, f32[8,1,16,128]{3,2,1,0:T(8,128)S(1)}, u32[]{:S(2)}) copy-start(f32[8,1,16,128]{3,2,1,0:T(8,128)S(1)} %get-tuple-element.12) | copy-start | bytes 196612
  66.2 0.7 %copy-start.6 = (f32[8,1,16,128]{3,2,1,0:T(8,128)}, f32[8,1,16,128]{3,2,1,0:T(8,128)S(1)}, u32[]{:S(2)}) copy-start(f32[8,1,16,128]{3,2,1,0:T(8,128)S(1)} %get-tuple-element.13) | copy-start | bytes 196612

commit v5 on v4

--- a/solution.py
+++ b/solution.py
@@ -34,25 +34,19 @@
     return rep_index(z_hi, y_high, y_one) * 32 + dp_index(x, z_two, z_one, core)
 
 
-SPREAD_X, SPREAD_Z, SPREAD_Y = (3, 2, 1, 0), (1, 0), (0, 1)
-FAR_TWO, FAR_Z, FAR_Y = (0, 1), (1, 0), (2, 3, 0, 1)
-GATHER_LOW, GATHER_HIGH = (0, 1), (2, 3, 0, 1)
-
-
-def spread_slot(x, z_one, y_one):
-    return SPREAD_X.index(x) * 4 + SPREAD_Z.index(z_one) * 2 + SPREAD_Y.index(y_one)
-
-
+SPREAD = [(x, z_one, y_one) for x in (3, 2, 1, 0) for z_one in (1, 0) for y_one in BITS]
+FAR = [(z_two, z_hi, y_high) for z_two in BITS for z_hi in (1, 0) for y_high in (2, 0, 3, 1)]
+GATHER_HIGH = (2, 3, 0, 1)
 SPREAD_GROUPS = [
-    [flat_index(x, z_two, z_one, core, z_hi, y_high, y_one) for x in SPREAD_X for z_one in SPREAD_Z for y_one in SPREAD_Y]
+    [flat_index(x, z_two, z_one, core, z_hi, y_high, y_one) for x, z_one, y_one in SPREAD]
     for z_hi in BITS for y_high in range(4) for z_two in BITS for core in BITS
 ]
 FAR_GROUPS = [
-    [flat_index(x, z_two, z_one, core, z_hi, y_high, y_one) for z_two in FAR_TWO for z_hi in FAR_Z for y_high in FAR_Y]
+    [flat_index(x, z_two, z_one, core, z_hi, y_high, y_one) for z_two, z_hi, y_high in FAR]
     for y_one in BITS for x in range(4) for z_one in BITS for core in BITS
 ]
 GATHER_GROUPS = [
-    [rep_index(z_hi, y_high, y_one) for y_one in GATHER_LOW for y_high in GATHER_HIGH] for z_hi in BITS
+    [rep_index(z_hi, y_high, y_one) for y_one in BITS for y_high in GATHER_HIGH] for z_hi in BITS
 ]
 CORE_PAIRS = [(d, d ^ 1) for d in range(32)]
 
@@ -93,8 +87,8 @@
     for copy in copies:
         copy.wait()
     for x, other_z, other_y in itertools.product(range(4), BITS, BITS):
-        peer = spread_slot(x, other_z, other_y)
-        start = base + x * (8 * SHARD) + other_z * (2 * SHARD) + GATHER_LOW.index(other_y) * (SHARD // 2)
+        peer = SPREAD.index((x, other_z, other_y))
+        start = base + x * (8 * SHARD) + other_z * (2 * SHARD) + other_y * (SHARD // 2)
         usable = (place >= -start) & (place < length - start)
         at = jnp.clip(start, -EIGHT, CAP) + EIGHT
         for i in range(3):
@@ -112,8 +106,8 @@
                 own = pl.multiple_of((block * 2 + core) * SHARD, SHARD)
                 total = taken_ref[pl.ds(block * SHARD, SHARD), :] + grad_ref[pl.ds(own, SHARD), :].astype(jnp.float32)
                 for y_one in BITS:
-                    peer = spread_slot(x, z_one, y_one)
-                    first = GATHER_LOW.index(y_one) * half
+                    peer = SPREAD.index((x, z_one, y_one))
+                    first = y_one * half
                     out_ref[peer, z_two * half : (z_two + 1) * half, :] = total[first : first + half]
     out_ref[:, SHARD:, :] = state_ref[...]
 
@@ -126,10 +120,10 @@
             total = in_ref[0, rows, :]
             for peer in range(1, 16):
                 total += in_ref[peer, rows, :]
-            source = spread_slot(turn // 2, turn % 2, 0), spread_slot(turn // 2, turn % 2, 1)
+            source = SPREAD.index((turn // 2, turn % 2, 0)), SPREAD.index((turn // 2, turn % 2, 1))
             state = in_ref[source[0], SHARD:, :] + in_ref[source[1], SHARD:, :]
             for z_hi in BITS:
-                slot = FAR_TWO.index(z_two) * 8 + z_hi * 4 + FAR_Y.index(y_high)
+                slot = FAR.index((z_two, z_hi, y_high))
                 out_ref[slot, :PIECE, :] = total
                 out_ref[slot, PIECE:, :] = state
 
@@ -168,8 +162,9 @@
     )(spread)
     far = lax.all_to_all(far, ("rep", "dp"), 0, 0, axis_index_groups=FAR_GROUPS)
     gradient = jnp.sum(far[:, :PIECE], axis=0)
-    state = jnp.sum(far[:, PIECE:].reshape(2, 8, 3, EIGHT, LANES), axis=1)
-    state = jnp.stack([state[FAR_TWO.index(z_two)] for z_two in BITS], axis=1).reshape(3, PIECE, LANES)
+    rows = far[:, PIECE:].reshape(16, 3, EIGHT, LANES)
+    halves = [sum(rows[i] for i in range(16) if FAR[i][0] == z_two) for z_two in BITS]
+    state = jnp.stack(halves, axis=1).reshape(3, PIECE, LANES)
     master, first, second = state
     first = BETA_ONE * first + (1.0 - BETA_ONE) * gradient
     second = BETA_TWO * second + (1.0 - BETA_TWO) * gradient * gradient

time: 67.2 us -> 66.6 us (level)
  no operation moved by 1% of the time
where the time goes in v5:
time: 66.6 us; the launch traced here: 66.3 us
  blocking collectives  58.6 us (88%)
  starting transfers between devices  2.05 us (3%)
  between operations  1.54 us (2%)
  local copies, waits for them, and re-layouts  1.22 us (2%)
  waiting for transfers between devices  1.11 us (2%)
  Pallas kernels  0.9 us (1%)
  other arithmetic  0.88 us (1%)
    all_to_all x1, blocking collectives, local(): lax.all_to_all(spread, ('rep', 'dp'), 0, 0, axis_index_groups=SPREAD_GROUPS)  25.8 us
    all_to_all x1, blocking collectives, local(): far = lax.all_to_all(far, ('rep', 'dp'), 0, 0, axis_index_groups=FAR_GROUPS)  20.4 us
    all_to_all x1, blocking collectives, local(): rows = lax.all_to_all(rows, 'rep', 0, 0, axis_index_groups=GATHER_GROUPS)  12.4 us
    ppermute x1, starting transfers between devices, local(): lax.ppermute(given.astype(jnp.float32).reshape(16 * SHARD, LANES), 'dp',...  2.05 us
  transfers between devices with their start and end apart: 1, of which 1 were waited for; matrix products, arithmetic and copies ran while one was open for 0% of the time, Pallas kernels for 1%

profile of v5, /device:TPU:8, one launch (start us, length us, event | category | flops | bytes accessed | tf_op | source)
XLA Modules:
  0.0 66.3 jit_solution(18320306136415192190)
XLA Ops:
  0.6 0.0 copy-start.1
  0.7 0.0 copy-start.2
  0.7 0.0 copy-start.3
  0.7 0.0 copy-start.4
  0.7 1.2 %constant_dynamic-slice_fusion = bf16[16,1,128,128]{3,2,1,0:T(8,128)(2,1)S(1)} fusion(bf16[16,2,128,128]{3,2,1,0:T(8,128)(2,1)} %bitcast.41, s32[]{:T(128)S(6)} %select_n.12), kind=kLoop, calls=%fused_computation.40 | loop fusion | bytes 1048580 | tf_op jit(solution)/shard_map/jit(dynamic_index_in_dim)/dynamic_slice | solution.py:134
  1.8 0.0 copy-start
  1.9 0.1 bitcast_convert_fusion
  2.0 2.1 %collective-permute-start = (f32[2048,128]{1,0:T(8,128)S(1)}, f32[2048,128]{1,0:T(8,128)S(1)}, u32[]{:S(2)}, u32[]{:S(2)}) collective-permute-start(f32[2048,128]{1,0:T(8,128)S(1)} %bitcast_convert_fusion), channel_id=1, source_target_pairs={{0,1},{1,0},{2,3},{3,2},{4,5},{5,4},{6,7},{7,6},{8,9},{9,8},{10,11... | collective-permute-start | bytes 3145736 | tf_op jit(solution)/shard_map/ppermute | solution.py:135
  4.0 0.0 copy-done.1
  4.0 0.0 copy-done.2
  4.0 0.0 copy-done.3
  4.1 0.0 copy-done.4
  4.1 0.7 %shard_map.93.state_ref = f32[16,24,128]{2,1,0:T(8,128)S(1)} custom-call(s32[16]{0:T(128)S(1)} %copy-done.4, f32[1,512,128]{2,1,0:T(8,128)S(1)} %copy-done.1, f32[1,512,128]{2,1,0:T(8,128)S(1)} %copy-done.2, f32[1,512,128]{2,1,0:T(8,128)S(1)} %copy-done.3), custom_call_target="tpu_custom_call" | custom-call | flops 100000 | bytes 1000000 | tf_op jit(solution)/shard_map/pallas_call | solution.py:137
  5.5 1.1 %collective-permute-done.taken_ref = f32[2048,128]{1,0:T(8,128)S(1)} collective-permute-done((f32[2048,128]{1,0:T(8,128)S(1)}, f32[2048,128]{1,0:T(8,128)S(1)}, u32[]{:S(2)}, u32[]{:S(2)}) %collective-permute-start) | collective-permute-done | bytes 1048608 | tf_op jit(solution)/shard_map/ppermute | solution.py:135
  6.7 0.0 copy-done
  6.7 0.1 shard_map.94
  6.8 25.8 %all_to_all.15.in_ref = f32[16,152,128]{2,1,0:T(8,128)S(1)} all-to-all(f32[16,152,128]{2,1,0:T(8,128)S(1)} %shard_map.94), channel_id=1, replica_groups={{26,58,24,56,18,50,16,48,10,42,8,40,2,34,0,32},{27,59,25,57,19,51,17,49..., dimensions={0} | all-to-all | bytes 2490368 | tf_op jit(solution)/shard_map/all_to_all | solution.py:155
  32.5 0.1 shard_map.95
  32.6 20.4 %all_to_all.16 = f32[16,40,128]{2,1,0:T(8,128)S(1)} all-to-all(f32[16,40,128]{2,1,0:T(8,128)S(1)} %shard_map.95), channel_id=1, replica_groups={{384,256,448,320,128,0,192,64,388,260,452,324,132,4,196,68},{385,257,44..., dimensions={0} | all-to-all | bytes 655360 | tf_op jit(solution)/shard_map/all_to_all | solution.py:163
  53.2 12.4 %all_to_all.17 = f32[8,3,16,128]{3,2,1,0:T(8,128)S(1)} all-to-all(f32[8,3,16,128]{3,2,1,0:T(8,128)S(1)} %broadcast_in_dim.3), channel_id=1, replica_groups={{128,192,0,64,160,224,32,96},{384,448,256,320,416,480,288,352},{129,193..., dimensions={0} | all-to-all | bytes 393216 | tf_op jit(solution)/shard_map/all_to_all | solution.py:172
  65.6 0.0 copy-start.5
  65.6 0.0 copy-start.6
  65.6 0.7 %bitcast_subtract_fusion = (f32[128,128]{1,0:T(8,128)}, f32[128,128]{1,0:T(8,128)}) fusion(f32[8,1,16,128]{3,2,1,0:T(8,128)S(1)} %get-tuple-element.16, f32[]{:T(128)} %bitcast.3, f32[]{:T(128)} %bitcast.2, f32[8,1,16,128]{3,2,1,0:T(8,128)S(1)} %get-tuple-element.14, f32[8,1,16,128]{3,2,1,0:T(8,128)S(1)} %get-tuple-element.15), kind=kLoop, calls=%fused_computation.2 | loop fusion | flops 131072 | bytes 327688 | tf_op jit(solution)/shard_map/sub | solution.py:175
  66.3 0.0 copy-done.5
  (8 shorter events, 0.1 us)
Async XLA Ops:
  0.6 3.4 %copy-start.1 = (f32[1,512,128]{2,1,0:T(8,128)S(1)}, f32[1,512,128]{2,1,0:T(8,128)}, u32[]{:S(2)}) copy-start(f32[1,512,128]{2,1,0:T(8,128)} %master_ref.1) | copy-start | bytes 786436
  0.7 3.4 %copy-start.2 = (f32[1,512,128]{2,1,0:T(8,128)S(1)}, f32[1,512,128]{2,1,0:T(8,128)}, u32[]{:S(2)}) copy-start(f32[1,512,128]{2,1,0:T(8,128)} %first_ref.1) | copy-start | bytes 786436
  0.7 3.4 %copy-start.3 = (f32[1,512,128]{2,1,0:T(8,128)S(1)}, f32[1,512,128]{2,1,0:T(8,128)}, u32[]{:S(2)}) copy-start(f32[1,512,128]{2,1,0:T(8,128)} %second_ref.1) | copy-start | bytes 786436
  0.7 3.4 %copy-start.4 = (s32[16]{0:T(128)S(1)}, s32[16]{0:T(128)}, u32[]{:S(2)}) copy-start(s32[16]{0:T(128)} %rows_ref.1) | copy-start | bytes 196
  1.8 4.8 %copy-start = (bf16[1,1,4096,128]{3,2,1,0:T(8,128)(2,1)S(1)}, bf16[1,1,4096,128]{3,2,1,0:T(8,128)(2,1)}, u32[]{:S(2)}) copy-start(bf16[1,1,4096,128]{3,2,1,0:T(8,128)(2,1)} %param.9) | copy-start | bytes 3145732
  2.0 4.7 %collective-permute-start = (f32[2048,128]{1,0:T(8,128)S(1)}, f32[2048,128]{1,0:T(8,128)S(1)}, u32[]{:S(2)}, u32[]{:S(2)}) collective-permute-start(f32[2048,128]{1,0:T(8,128)S(1)} %bitcast_convert_fusion), channel_id=1, source_target_pairs={{0,1},{1,0},{2,3},{3,2},{4,5},{5,4},{6,7},{7,6},{8,9},{9,8},{10,11... | collective-permute-start | bytes 3145736 | tf_op jit(solution)/shard_map/ppermute | solution.py:135
  65.6 0.7 %copy-start.5 = (f32[8,1,16,128]{3,2,1,0:T(8,128)}, f32[8,1,16,128]{3,2,1,0:T(8,128)S(1)}, u32[]{:S(2)}) copy-start(f32[8,1,16,128]{3,2,1,0:T(8,128)S(1)} %get-tuple-element.14) | copy-start | bytes 196612
  65.6 0.7 %copy-start.6 = (f32[8,1,16,128]{3,2,1,0:T(8,128)}, f32[8,1,16,128]{3,2,1,0:T(8,128)S(1)}, u32[]{:S(2)}) copy-start(f32[8,1,16,128]{3,2,1,0:T(8,128)S(1)} %get-tuple-element.15) | copy-start | bytes 196612

commit v6 on v5

--- a/solution.py
+++ b/solution.py
@@ -36,7 +36,7 @@
 
 SPREAD = [(x, z_one, y_one) for x in (3, 2, 1, 0) for z_one in (1, 0) for y_one in BITS]
 FAR = [(z_two, z_hi, y_high) for z_two in BITS for z_hi in (1, 0) for y_high in (2, 0, 3, 1)]
-GATHER_HIGH = (2, 3, 0, 1)
+GATHER_HIGH = (2, 0, 3, 1)
 SPREAD_GROUPS = [
     [flat_index(x, z_two, z_one, core, z_hi, y_high, y_one) for x, z_one, y_one in SPREAD]
     for z_hi in BITS for y_high in range(4) for z_two in BITS for core in BITS
@@ -46,7 +46,7 @@
     for y_one in BITS for x in range(4) for z_one in BITS for core in BITS
 ]
 GATHER_GROUPS = [
-    [rep_index(z_hi, y_high, y_one) for y_one in BITS for y_high in GATHER_HIGH] for z_hi in BITS
+    [rep_index(z_hi, y_high, y_one) for y_high in GATHER_HIGH for y_one in BITS] for z_hi in BITS
 ]
 CORE_PAIRS = [(d, d ^ 1) for d in range(32)]
 
@@ -82,13 +82,13 @@
         begin += jnp.where(owner < rank_rep, held_rows, 0)
         length += jnp.where(owner == rank_rep, held_rows, 0)
     piece = sum(jnp.where(turn % 4 == y_high, GATHER_HIGH.index(y_high), 0) for y_high in range(4))
-    base = (turn // 4) * (4 * SHARD) + core * SHARD + piece * PIECE + z_two * EIGHT - begin
+    base = (turn // 4) * (4 * SHARD) + core * SHARD + piece * (2 * PIECE) + z_two * EIGHT - begin
     place = lax.broadcasted_iota(jnp.int32, (EIGHT, LANES), 0)
     for copy in copies:
         copy.wait()
     for x, other_z, other_y in itertools.product(range(4), BITS, BITS):
         peer = SPREAD.index((x, other_z, other_y))
-        start = base + x * (8 * SHARD) + other_z * (2 * SHARD) + other_y * (SHARD // 2)
+        start = base + x * (8 * SHARD) + other_z * (2 * SHARD) + other_y * PIECE
         usable = (place >= -start) & (place < length - start)
         at = jnp.clip(start, -EIGHT, CAP) + EIGHT
         for i in range(3):
@@ -107,8 +107,9 @@
                 total = taken_ref[pl.ds(block * SHARD, SHARD), :] + grad_ref[pl.ds(own, SHARD), :].astype(jnp.float32)
                 for y_one in BITS:
                     peer = SPREAD.index((x, z_one, y_one))
-                    first = y_one * half
-                    out_ref[peer, z_two * half : (z_two + 1) * half, :] = total[first : first + half]
+                    for turn in range(4):
+                        first, to = (2 * turn + y_one) * PIECE, z_two * half + turn * PIECE
+                        out_ref[peer, to : to + PIECE, :] = total[first : first + PIECE]
     out_ref[:, SHARD:, :] = state_ref[...]
 
 

time: 66.6 us -> 66.5 us (level)
  the two profiles are of different devices: /device:TPU:8 before, /device:TPU:16 now
where the time goes in v6:
time: 66.5 us; the launch traced here: 66.2 us
  blocking collectives  58.5 us (88%)
  starting transfers between devices  2.05 us (3%)
  between operations  1.54 us (2%)
  local copies, waits for them, and re-layouts  1.22 us (2%)
  waiting for transfers between devices  1.11 us (2%)
  Pallas kernels  0.9 us (1%)
  other arithmetic  0.88 us (1%)
    all_to_all x1, blocking collectives, local(): lax.all_to_all(spread, ('rep', 'dp'), 0, 0, axis_index_groups=SPREAD_GROUPS)  24 us
    all_to_all x1, blocking collectives, local(): far = lax.all_to_all(far, ('rep', 'dp'), 0, 0, axis_index_groups=FAR_GROUPS)  22.6 us
    all_to_all x1, blocking collectives, local(): rows = lax.all_to_all(rows, 'rep', 0, 0, axis_index_groups=GATHER_GROUPS)  12 us
    ppermute x1, starting transfers between devices, local(): lax.ppermute(given.astype(jnp.float32).reshape(16 * SHARD, LANES), 'dp',...  2.05 us
  transfers between devices with their start and end apart: 1, of which 1 were waited for; matrix products, arithmetic and copies ran while one was open for 0% of the time, Pallas kernels for 1%

profile of v6, /device:TPU:16, one launch (start us, length us, event | category | flops | bytes accessed | tf_op | source)
XLA Modules:
  0.0 66.2 jit_solution(18264721232272813883)
XLA Ops:
  0.6 0.0 copy-start.1
  0.7 0.0 copy-start.2
  0.7 0.0 copy-start.3
  0.7 0.0 copy-start.4
  0.7 1.2 %constant_dynamic-slice_fusion = bf16[16,1,128,128]{3,2,1,0:T(8,128)(2,1)S(1)} fusion(bf16[16,2,128,128]{3,2,1,0:T(8,128)(2,1)} %bitcast.41, s32[]{:T(128)S(6)} %select_n.12), kind=kLoop, calls=%fused_computation.40 | loop fusion | bytes 1048580 | tf_op jit(solution)/shard_map/jit(dynamic_index_in_dim)/dynamic_slice | solution.py:135
  1.8 0.0 copy-start
  1.9 0.1 bitcast_convert_fusion
  2.0 2.1 %collective-permute-start = (f32[2048,128]{1,0:T(8,128)S(1)}, f32[2048,128]{1,0:T(8,128)S(1)}, u32[]{:S(2)}, u32[]{:S(2)}) collective-permute-start(f32[2048,128]{1,0:T(8,128)S(1)} %bitcast_convert_fusion), channel_id=1, source_target_pairs={{0,1},{1,0},{2,3},{3,2},{4,5},{5,4},{6,7},{7,6},{8,9},{9,8},{10,11... | collective-permute-start | bytes 3145736 | tf_op jit(solution)/shard_map/ppermute | solution.py:136
  4.0 0.0 copy-done.1
  4.0 0.0 copy-done.2
  4.0 0.0 copy-done.3
  4.1 0.0 copy-done.4
  4.1 0.7 %shard_map.93.state_ref = f32[16,24,128]{2,1,0:T(8,128)S(1)} custom-call(s32[16]{0:T(128)S(1)} %copy-done.4, f32[1,512,128]{2,1,0:T(8,128)S(1)} %copy-done.1, f32[1,512,128]{2,1,0:T(8,128)S(1)} %copy-done.2, f32[1,512,128]{2,1,0:T(8,128)S(1)} %copy-done.3), custom_call_target="tpu_custom_call" | custom-call | flops 100000 | bytes 1000000 | tf_op jit(solution)/shard_map/pallas_call | solution.py:138
  5.5 1.1 %collective-permute-done.taken_ref = f32[2048,128]{1,0:T(8,128)S(1)} collective-permute-done((f32[2048,128]{1,0:T(8,128)S(1)}, f32[2048,128]{1,0:T(8,128)S(1)}, u32[]{:S(2)}, u32[]{:S(2)}) %collective-permute-start) | collective-permute-done | bytes 1048608 | tf_op jit(solution)/shard_map/ppermute | solution.py:136
  6.7 0.0 copy-done
  6.7 0.1 shard_map.94
  6.8 24.0 %all_to_all.15.in_ref = f32[16,152,128]{2,1,0:T(8,128)S(1)} all-to-all(f32[16,152,128]{2,1,0:T(8,128)S(1)} %shard_map.94), channel_id=1, replica_groups={{26,58,24,56,18,50,16,48,10,42,8,40,2,34,0,32},{27,59,25,57,19,51,17,49..., dimensions={0} | all-to-all | bytes 2490368 | tf_op jit(solution)/shard_map/all_to_all | solution.py:156
  30.8 0.1 shard_map.95
  30.8 22.6 %all_to_all.16 = f32[16,40,128]{2,1,0:T(8,128)S(1)} all-to-all(f32[16,40,128]{2,1,0:T(8,128)S(1)} %shard_map.95), channel_id=1, replica_groups={{384,256,448,320,128,0,192,64,388,260,452,324,132,4,196,68},{385,257,44..., dimensions={0} | all-to-all | bytes 655360 | tf_op jit(solution)/shard_map/all_to_all | solution.py:164
  53.5 12.0 %all_to_all.17 = f32[8,3,16,128]{3,2,1,0:T(8,128)S(1)} all-to-all(f32[8,3,16,128]{3,2,1,0:T(8,128)S(1)} %broadcast_in_dim.3), channel_id=1, replica_groups={{128,160,0,32,192,224,64,96},{384,416,256,288,448,480,320,352},{129,161..., dimensions={0} | all-to-all | bytes 393216 | tf_op jit(solution)/shard_map/all_to_all | solution.py:173
  65.5 0.0 copy-start.5
  65.5 0.0 copy-start.6
  65.5 0.7 %bitcast_subtract_fusion = (f32[128,128]{1,0:T(8,128)}, f32[128,128]{1,0:T(8,128)}) fusion(f32[8,1,16,128]{3,2,1,0:T(8,128)S(1)} %get-tuple-element.16, f32[]{:T(128)} %bitcast.3, f32[]{:T(128)} %bitcast.2, f32[8,1,16,128]{3,2,1,0:T(8,128)S(1)} %get-tuple-element.14, f32[8,1,16,128]{3,2,1,0:T(8,128)S(1)} %get-tuple-element.15), kind=kLoop, calls=%fused_computation.2 | loop fusion | flops 131072 | bytes 327688 | tf_op jit(solution)/shard_map/sub | solution.py:176
  66.2 0.0 copy-done.5
  (8 shorter events, 0.1 us)
Async XLA Ops:
  0.6 3.4 %copy-start.1 = (f32[1,512,128]{2,1,0:T(8,128)S(1)}, f32[1,512,128]{2,1,0:T(8,128)}, u32[]{:S(2)}) copy-start(f32[1,512,128]{2,1,0:T(8,128)} %master_ref.1) | copy-start | bytes 786436
  0.7 3.4 %copy-start.2 = (f32[1,512,128]{2,1,0:T(8,128)S(1)}, f32[1,512,128]{2,1,0:T(8,128)}, u32[]{:S(2)}) copy-start(f32[1,512,128]{2,1,0:T(8,128)} %first_ref.1) | copy-start | bytes 786436
  0.7 3.4 %copy-start.3 = (f32[1,512,128]{2,1,0:T(8,128)S(1)}, f32[1,512,128]{2,1,0:T(8,128)}, u32[]{:S(2)}) copy-start(f32[1,512,128]{2,1,0:T(8,128)} %second_ref.1) | copy-start | bytes 786436
  0.7 3.4 %copy-start.4 = (s32[16]{0:T(128)S(1)}, s32[16]{0:T(128)}, u32[]{:S(2)}) copy-start(s32[16]{0:T(128)} %rows_ref.1) | copy-start | bytes 196
  1.8 4.8 %copy-start = (bf16[1,1,4096,128]{3,2,1,0:T(8,128)(2,1)S(1)}, bf16[1,1,4096,128]{3,2,1,0:T(8,128)(2,1)}, u32[]{:S(2)}) copy-start(bf16[1,1,4096,128]{3,2,1,0:T(8,128)(2,1)} %param.9) | copy-start | bytes 3145732
  2.0 4.7 %collective-permute-start = (f32[2048,128]{1,0:T(8,128)S(1)}, f32[2048,128]{1,0:T(8,128)S(1)}, u32[]{:S(2)}, u32[]{:S(2)}) collective-permute-start(f32[2048,128]{1,0:T(8,128)S(1)} %bitcast_convert_fusion), channel_id=1, source_target_pairs={{0,1},{1,0},{2,3},{3,2},{4,5},{5,4},{6,7},{7,6},{8,9},{9,8},{10,11... | collective-permute-start | bytes 3145736 | tf_op jit(solution)/shard_map/ppermute | solution.py:136
  65.5 0.7 %copy-start.5 = (f32[8,1,16,128]{3,2,1,0:T(8,128)}, f32[8,1,16,128]{3,2,1,0:T(8,128)S(1)}, u32[]{:S(2)}) copy-start(f32[8,1,16,128]{3,2,1,0:T(8,128)S(1)} %get-tuple-element.14) | copy-start | bytes 196612
  65.5 0.7 %copy-start.6 = (f32[8,1,16,128]{3,2,1,0:T(8,128)}, f32[8,1,16,128]{3,2,1,0:T(8,128)S(1)}, u32[]{:S(2)}) copy-start(f32[8,1,16,128]{3,2,1,0:T(8,128)S(1)} %get-tuple-element.15) | copy-start | bytes 196612

commit v7 on v6

--- a/solution.py
+++ b/solution.py
@@ -35,7 +35,7 @@
 
 
 SPREAD = [(x, z_one, y_one) for x in (3, 2, 1, 0) for z_one in (1, 0) for y_one in BITS]
-FAR = [(z_two, z_hi, y_high) for z_two in BITS for z_hi in (1, 0) for y_high in (2, 0, 3, 1)]
+FAR = [(z_two, z_hi, y_high) for z_two in BITS for y_high in (2, 0, 3, 1) for z_hi in (1, 0)]
 GATHER_HIGH = (2, 0, 3, 1)
 SPREAD_GROUPS = [
     [flat_index(x, z_two, z_one, core, z_hi, y_high, y_one) for x, z_one, y_one in SPREAD]

time: 66.5 us -> 66.6 us (level)
  the two profiles are of different devices: /device:TPU:16 before, /device:TPU:22 now
where the time goes in v7:
time: 66.6 us; the launch traced here: 66.3 us
  blocking collectives  58.6 us (88%)
  starting transfers between devices  2.05 us (3%)
  between operations  1.54 us (2%)
  local copies, waits for them, and re-layouts  1.22 us (2%)
  waiting for transfers between devices  1.11 us (2%)
  Pallas kernels  0.9 us (1%)
  other arithmetic  0.88 us (1%)
    all_to_all x1, blocking collectives, local(): lax.all_to_all(spread, ('rep', 'dp'), 0, 0, axis_index_groups=SPREAD_GROUPS)  23.3 us
    all_to_all x1, blocking collectives, local(): far = lax.all_to_all(far, ('rep', 'dp'), 0, 0, axis_index_groups=FAR_GROUPS)  23 us
    all_to_all x1, blocking collectives, local(): rows = lax.all_to_all(rows, 'rep', 0, 0, axis_index_groups=GATHER_GROUPS)  12.3 us
    ppermute x1, starting transfers between devices, local(): lax.ppermute(given.astype(jnp.float32).reshape(16 * SHARD, LANES), 'dp',...  2.05 us
  transfers between devices with their start and end apart: 1, of which 1 were waited for; matrix products, arithmetic and copies ran while one was open for 0% of the time, Pallas kernels for 1%

profile of v7, /device:TPU:22, one launch (start us, length us, event | category | flops | bytes accessed | tf_op | source)
XLA Modules:
  0.0 66.3 jit_solution(10567925363717070257)
XLA Ops:
  0.6 0.0 copy-start.1
  0.7 0.0 copy-start.2
  0.7 0.0 copy-start.3
  0.7 0.0 copy-start.4
  0.7 1.2 %constant_dynamic-slice_fusion = bf16[16,1,128,128]{3,2,1,0:T(8,128)(2,1)S(1)} fusion(bf16[16,2,128,128]{3,2,1,0:T(8,128)(2,1)} %bitcast.41, s32[]{:T(128)S(6)} %select_n.12), kind=kLoop, calls=%fused_computation.40 | loop fusion | bytes 1048580 | tf_op jit(solution)/shard_map/jit(dynamic_index_in_dim)/dynamic_slice | solution.py:135
  1.8 0.0 copy-start
  1.9 0.1 bitcast_convert_fusion
  2.0 2.1 %collective-permute-start = (f32[2048,128]{1,0:T(8,128)S(1)}, f32[2048,128]{1,0:T(8,128)S(1)}, u32[]{:S(2)}, u32[]{:S(2)}) collective-permute-start(f32[2048,128]{1,0:T(8,128)S(1)} %bitcast_convert_fusion), channel_id=1, source_target_pairs={{0,1},{1,0},{2,3},{3,2},{4,5},{5,4},{6,7},{7,6},{8,9},{9,8},{10,11... | collective-permute-start | bytes 3145736 | tf_op jit(solution)/shard_map/ppermute | solution.py:136
  4.0 0.0 copy-done.1
  4.0 0.0 copy-done.2
  4.0 0.0 copy-done.3
  4.1 0.0 copy-done.4
  4.1 0.7 %shard_map.93.state_ref = f32[16,24,128]{2,1,0:T(8,128)S(1)} custom-call(s32[16]{0:T(128)S(1)} %copy-done.4, f32[1,512,128]{2,1,0:T(8,128)S(1)} %copy-done.1, f32[1,512,128]{2,1,0:T(8,128)S(1)} %copy-done.2, f32[1,512,128]{2,1,0:T(8,128)S(1)} %copy-done.3), custom_call_target="tpu_custom_call" | custom-call | flops 100000 | bytes 1000000 | tf_op jit(solution)/shard_map/pallas_call | solution.py:138
  5.5 1.1 %collective-permute-done.taken_ref = f32[2048,128]{1,0:T(8,128)S(1)} collective-permute-done((f32[2048,128]{1,0:T(8,128)S(1)}, f32[2048,128]{1,0:T(8,128)S(1)}, u32[]{:S(2)}, u32[]{:S(2)}) %collective-permute-start) | collective-permute-done | bytes 1048608 | tf_op jit(solution)/shard_map/ppermute | solution.py:136
  6.7 0.0 copy-done
  6.7 0.1 shard_map.94
  6.8 23.3 %all_to_all.15.in_ref = f32[16,152,128]{2,1,0:T(8,128)S(1)} all-to-all(f32[16,152,128]{2,1,0:T(8,128)S(1)} %shard_map.94), channel_id=1, replica_groups={{26,58,24,56,18,50,16,48,10,42,8,40,2,34,0,32},{27,59,25,57,19,51,17,49..., dimensions={0} | all-to-all | bytes 2490368 | tf_op jit(solution)/shard_map/all_to_all | solution.py:156
  30.1 0.1 shard_map.95
  30.2 23.0 %all_to_all.16 = f32[16,40,128]{2,1,0:T(8,128)S(1)} all-to-all(f32[16,40,128]{2,1,0:T(8,128)S(1)} %shard_map.95), channel_id=1, replica_groups={{384,128,256,0,448,192,320,64,388,132,260,4,452,196,324,68},{385,129,25..., dimensions={0} | all-to-all | bytes 655360 | tf_op jit(solution)/shard_map/all_to_all | solution.py:164
  53.3 12.3 %all_to_all.17 = f32[8,3,16,128]{3,2,1,0:T(8,128)S(1)} all-to-all(f32[8,3,16,128]{3,2,1,0:T(8,128)S(1)} %broadcast_in_dim.3), channel_id=1, replica_groups={{128,160,0,32,192,224,64,96},{384,416,256,288,448,480,320,352},{129,161..., dimensions={0} | all-to-all | bytes 393216 | tf_op jit(solution)/shard_map/all_to_all | solution.py:173
  65.6 0.0 copy-start.5
  65.6 0.0 copy-start.6
  65.6 0.7 %bitcast_subtract_fusion = (f32[128,128]{1,0:T(8,128)}, f32[128,128]{1,0:T(8,128)}) fusion(f32[8,1,16,128]{3,2,1,0:T(8,128)S(1)} %get-tuple-element.16, f32[]{:T(128)} %bitcast.3, f32[]{:T(128)} %bitcast.2, f32[8,1,16,128]{3,2,1,0:T(8,128)S(1)} %get-tuple-element.14, f32[8,1,16,128]{3,2,1,0:T(8,128)S(1)} %get-tuple-element.15), kind=kLoop, calls=%fused_computation.2 | loop fusion | flops 131072 | bytes 327688 | tf_op jit(solution)/shard_map/sub | solution.py:176
  66.3 0.0 copy-done.5
  (8 shorter events, 0.1 us)
Async XLA Ops:
  0.6 3.4 %copy-start.1 = (f32[1,512,128]{2,1,0:T(8,128)S(1)}, f32[1,512,128]{2,1,0:T(8,128)}, u32[]{:S(2)}) copy-start(f32[1,512,128]{2,1,0:T(8,128)} %master_ref.1) | copy-start | bytes 786436
  0.7 3.4 %copy-start.2 = (f32[1,512,128]{2,1,0:T(8,128)S(1)}, f32[1,512,128]{2,1,0:T(8,128)}, u32[]{:S(2)}) copy-start(f32[1,512,128]{2,1,0:T(8,128)} %first_ref.1) | copy-start | bytes 786436
  0.7 3.4 %copy-start.3 = (f32[1,512,128]{2,1,0:T(8,128)S(1)}, f32[1,512,128]{2,1,0:T(8,128)}, u32[]{:S(2)}) copy-start(f32[1,512,128]{2,1,0:T(8,128)} %second_ref.1) | copy-start | bytes 786436
  0.7 3.4 %copy-start.4 = (s32[16]{0:T(128)S(1)}, s32[16]{0:T(128)}, u32[]{:S(2)}) copy-start(s32[16]{0:T(128)} %rows_ref.1) | copy-start | bytes 196
  1.8 4.8 %copy-start = (bf16[1,1,4096,128]{3,2,1,0:T(8,128)(2,1)S(1)}, bf16[1,1,4096,128]{3,2,1,0:T(8,128)(2,1)}, u32[]{:S(2)}) copy-start(bf16[1,1,4096,128]{3,2,1,0:T(8,128)(2,1)} %param.9) | copy-start | bytes 3145732
  2.0 4.7 %collective-permute-start = (f32[2048,128]{1,0:T(8,128)S(1)}, f32[2048,128]{1,0:T(8,128)S(1)}, u32[]{:S(2)}, u32[]{:S(2)}) collective-permute-start(f32[2048,128]{1,0:T(8,128)S(1)} %bitcast_convert_fusion), channel_id=1, source_target_pairs={{0,1},{1,0},{2,3},{3,2},{4,5},{5,4},{6,7},{7,6},{8,9},{9,8},{10,11... | collective-permute-start | bytes 3145736 | tf_op jit(solution)/shard_map/ppermute | solution.py:136
  65.6 0.7 %copy-start.5 = (f32[8,1,16,128]{3,2,1,0:T(8,128)}, f32[8,1,16,128]{3,2,1,0:T(8,128)S(1)}, u32[]{:S(2)}) copy-start(f32[8,1,16,128]{3,2,1,0:T(8,128)S(1)} %get-tuple-element.14) | copy-start | bytes 196612
  65.6 0.7 %copy-start.6 = (f32[8,1,16,128]{3,2,1,0:T(8,128)}, f32[8,1,16,128]{3,2,1,0:T(8,128)S(1)}, u32[]{:S(2)}) copy-start(f32[8,1,16,128]{3,2,1,0:T(8,128)S(1)} %get-tuple-element.15) | copy-start | bytes 196612
